TPU v7x, 32 devices: a whole 2x2x4 slice. The times are simulated.
32 devices in a mesh: row: 8 (over z, core), col: 4 (over y, x), rep: 1.
Axes of the slice: x: 2, y: 2, z: 4, core: 2. Of those that a mesh axis runs over, the one named last changes fastest.
Arguments:
- momentum: float32 [1, 8192, 8192], P('rep', 'row', 'col'), may hold values from -6 to 6
- gradient: bfloat16 [1, 8192, 8192], P('rep', 'row', 'col'), may hold values from -6 to 6
- weight: float32 [8192, 8192], P('row', 'col'), may hold values from -0.0625 to 0.0625
- right_basis: float32 [8192, 256], P('col'), may hold values from -6 to 6
Outputs:
- new_momentum: float32 [1, 8192, 8192], P('rep', 'row', 'col')
- new_weight: float32 [8192, 8192], P('row', 'col')
- new_basis: float32 [8192, 256], P('col')
All inputs are finite; a program needn't handle non-finite values.
Results may differ from a plain program's by a relative error of at most 0.0012.
Values sent between devices are 32-bit elements; how exact they have to be, the bound alone decides.
No kernel may reach another device: no remote copies, remote signals or barrier semaphores. Data moves between devices by JAX's collectives and lax.ppermute only.
A program may use at most 128 MiB of HBM per device.

v0:
```python
import functools

import jax
import jax.numpy as jnp
from jax import lax
from jax.experimental import pallas as pl
from jax.experimental.pallas import tpu as pltpu
from jax.sharding import PartitionSpec as P

D = 8192
RANK = 256
ITERS = 2
HALF = RANK // 2
QUARTER = RANK // 4
PART = RANK // 8
SUB = 8
TILE = 256
STEP = 512

beta_mom = 0.95
learn_rate = 0.05

F32 = jnp.float32
BF16 = jnp.bfloat16
HIGHEST = lax.Precision.HIGHEST
HIGH = lax.Precision.HIGH
NT = ((1,), (1,))
NN = ((1,), (0,))


def dot(a, b, dims=NN, precision=None):
    return lax.dot_general(a, b, (dims, ((), ())), precision=precision, preferred_element_type=F32)


def split(x):
    high = x.astype(BF16)
    return high, (x - high.astype(F32)).astype(BF16)


def dot3(a, b, dims=NN):
    return dot(a[0], b[0], dims) + (dot(a[1], b[0], dims) + dot(a[0], b[1], dims))


def call(kernel, name, flops, moved, **rest):
    rest.setdefault("compiler_params", pltpu.CompilerParams(vmem_limit_bytes=24 * 2**20))
    return pl.pallas_call(
        kernel,
        name=name,
        cost_estimate=pl.CostEstimate(flops=flops, bytes_accessed=moved, transcendentals=0),
        **rest,
    )


def shaped(*shape, dtype=F32):
    return jax.ShapeDtypeStruct(shape, dtype)


VMEM = pl.BlockSpec(memory_space=pltpu.VMEM)
HBM = pl.BlockSpec(memory_space=pltpu.HBM)
SMEM = pl.BlockSpec(memory_space=pltpu.SMEM)


def inverse_factor(block):
    shape = (SUB, HALF)
    lanes = lax.broadcasted_iota(jnp.int32, shape, 1)
    subs = lax.broadcasted_iota(jnp.int32, shape, 0)
    count = HALF // SUB

    def spread(tile, lane):
        return jnp.broadcast_to(tile[:, lane:lane + 1], shape)

    def repeat(tile, sub):
        return jnp.broadcast_to(tile[sub:sub + 1, :], shape)

    tiles = [block[SUB * i:SUB * (i + 1), :] for i in range(count)]
    for t in range(count):
        low = SUB * t
        panel = jnp.logical_and(lanes >= low, lanes < low + SUB)
        cols = [spread(tiles[t], low + j) for j in range(SUB)]
        tile = jnp.where(panel, 0.0, tiles[t])
        scale, rows, upper = [], [], {}
        for j in range(SUB):
            r = lax.rsqrt(repeat(cols[j], j))
            mult = jnp.where(subs > j, cols[j] * r, 0.0)
            for k in range(j + 1, SUB):
                upper[j, k] = repeat(cols[k], j) * r
                cols[k] = cols[k] - mult * upper[j, k]
            row = jnp.where(lanes == low + j, r, repeat(tile, j) * r)
            tile = jnp.where(subs == j, row, tile - mult * row)
            scale.append(r)
            rows.append(row)
        tiles[t] = tile
        for i in range(t + 1, count):
            cols = [spread(tiles[i], low + j) for j in range(SUB)]
            tile = jnp.where(panel, 0.0, tiles[i])
            for j in range(SUB):
                mult = cols[j] * scale[j]
                for k in range(j + 1, SUB):
                    cols[k] = cols[k] - mult * upper[j, k]
                tile = tile - mult * rows[j]
            tiles[i] = tile
    full = jnp.concatenate(tiles, axis=0)
    down = lax.broadcasted_iota(jnp.int32, (HALF, HALF), 0)
    across = lax.broadcasted_iota(jnp.int32, (HALF, HALF), 1)
    return jnp.where(across <= down, full, 0.0)


def inverse_body(gram_ref, out_ref):
    first = inverse_factor(gram_ref[:HALF, :HALF])
    side = dot(gram_ref[HALF:, :HALF], first, NT, HIGHEST)
    rest = gram_ref[HALF:, HALF:] - dot(side, side, NT, HIGHEST)
    second = inverse_factor(rest)
    out_ref[:HALF, :HALF] = first
    out_ref[:HALF, HALF:] = jnp.zeros((HALF, HALF), F32)
    out_ref[HALF:, :HALF] = -dot(second, dot(side, first, precision=HIGHEST), precision=HIGHEST)
    out_ref[HALF:, HALF:] = second


def inverse_cholesky(gram):
    return call(
        inverse_body, "inverse_cholesky", 12_000_000_000, 2 * 4 * RANK * RANK,
        out_shape=shaped(RANK, RANK), in_specs=[VMEM], out_specs=VMEM,
    )(gram)


def place(out_ref, me, mine, other):
    for b in range(4):
        block = (mine, other)[b // 2][PART * (b % 2):PART * (b % 2 + 1), :]
        out_ref[pl.ds(pl.multiple_of((me ^ b) * PART, PART), PART), :] = block


def start_kernel(me_ref, momentum_ref, gradient_ref, basis_ref, high_ref, low_ref, up_ref, down_ref, second_ref):
    rows, cols = momentum_ref.shape
    half = rows // 2

    def body(momentum, gradient, basis):
        step = pl.program_id(0)
        here = pl.ds(pl.multiple_of(step * STEP, STEP), STEP)
        bhigh, blow = split(basis[...])
        second_ref[here, :HALF], second_ref[here, HALF:] = bhigh[:, HALF:], blow[:, HALF:]
        high, low = split(momentum[...] + gradient[...].astype(F32))
        high_ref[:, here], low_ref[:, here] = high, low
        both = dot(high, jnp.concatenate([bhigh[:, :HALF], blow[:, :HALF]], axis=1))
        part = (both[:, :HALF] + both[:, HALF:]) + dot(low, bhigh[:, :HALF])

        @pl.when(step == 0)
        def _():
            up_ref[...] = part[:half]
            down_ref[...] = part[half:]

        @pl.when(step > 0)
        def _():
            up_ref[...] += part[:half]
            down_ref[...] += part[half:]

    block = pl.BlockSpec((rows, STEP), lambda i: (0, i))
    pltpu.emit_pipeline(
        body, grid=(cols // STEP,), in_specs=[block, block, pl.BlockSpec((STEP, RANK), lambda i: (i, 0))],
    )(momentum_ref, gradient_ref, basis_ref)


def start(me, *args):
    rows, cols = args[0].shape
    return call(
        start_kernel, "start", 4 * rows * cols * RANK, 6 * rows * cols,
        out_shape=[pltpu.VMEM((rows, cols), BF16)] * 2 + [shaped(rows // 2, HALF)] * 2 + [shaped(cols, RANK, dtype=BF16)],
        in_specs=[SMEM] + [HBM] * 3, out_specs=[VMEM] * 5,
    )(me, *(pltpu.with_memory_space_constraint(x, pltpu.HBM) for x in args))


def left_kernel(dims, high_ref, low_ref, factor_ref, *refs):
    up_ref, down_ref = refs[-2:]
    half = down_ref.shape[0]

    @pl.loop(0, 2 * half // TILE)
    def _(c):
        here = pl.ds(pl.multiple_of(c * TILE, TILE), TILE)
        both = dot(high_ref[here, :], factor_ref[...], dims)
        fhigh = factor_ref[:HALF, :] if dims == NT else factor_ref[:, :HALF]
        part = (both[:, :HALF] + both[:, HALF:]) + dot(low_ref[here, :], fhigh, dims)
        there = pl.ds(pl.multiple_of(lax.rem(c * TILE, half), TILE), TILE)

        @pl.when(c < half // TILE)
        def _():
            up_ref[there, :] = part

        @pl.when(c >= half // TILE)
        def _():
            down_ref[there, :] = part

    if len(refs) == 3:
        up_ref[half:, :] = refs[0][...]


def left_product(buffer, factor, *square, dims=NT):
    rows, cols = buffer[0].shape
    return call(
        functools.partial(left_kernel, dims), "left", 0, 4 * rows * cols,
        out_shape=[shaped(rows // 2 + SUB * len(square), HALF), shaped(rows // 2, HALF)],
        in_specs=[VMEM] * (3 + len(square)), out_specs=[VMEM] * 2,
    )(*buffer, factor, *square)


def product_kernel(first, scaled, me_ref, *refs):
    before, refs = ((), refs) if first else (refs[:1], refs[1:])
    up, up_more, down, down_more, high_ref, low_ref, keep_ref, give_ref, left_ref, plain_ref, turned_ref, pair_ref = refs
    rows = down.shape[0]
    top, bottom = up[:rows, :] + up_more[:rows, :], down[...] + down_more[...]
    if scaled:
        total = up[rows:rows + 1, :] + up_more[rows:rows + 1, :]
        scale = 1.0 / jnp.sqrt(total / F32(D) + F32(1e-06))
        top, bottom = top * scale, bottom * scale
    left_ref[:rows, :] = top
    left_ref[rows:, :] = bottom
    plain_ref[:, :rows] = top.T
    plain_ref[:, rows:] = bottom.T
    me = me_ref[0]
    for b in range(4):
        block = plain_ref[pl.ds(pl.multiple_of((me ^ b) * PART, PART), PART), :]
        turned_ref[PART * b:PART * (b + 1), :] = block
        pair_ref[PART * b:PART * (b + 1), :], pair_ref[HALF + PART * b:HALF + PART * (b + 1), :] = split(block)
    spot = 0
    for ref in (*before, left_ref):
        gram = dot(turned_ref[...], ref[...], precision=HIGHEST)
        keep_ref[:, spot:spot + HALF] = gram[:QUARTER]
        give_ref[:, spot:spot + HALF] = gram[QUARTER:]
        spot += HALF
    step = 2 * TILE
    for c in range(high_ref.shape[1] // step):
        lanes = pl.ds(c * step, step)
        both = dot(pair_ref[...], high_ref[:, lanes])
        part = (both[:HALF] + both[HALF:]) + dot(pair_ref[:HALF, :], low_ref[:, lanes])
        lanes = pl.ds(spot + c * step, step)
        keep_ref[:, lanes] = part[:QUARTER]
        give_ref[:, lanes] = part[QUARTER:]


def product(scaled, me, before, parts, buffer):
    rows, cols = buffer[0].shape
    width = HALF * (len(before) + 1) + cols
    return call(
        functools.partial(product_kernel, not before, scaled), "product", 4 * rows * width * RANK, 4 * rows * width,
        out_shape=[shaped(QUARTER, width)] * 2 + [shaped(rows, HALF)],
        in_specs=[SMEM] + [VMEM] * (6 + len(before)), out_specs=[VMEM] * 3,
        scratch_shapes=[pltpu.VMEM((HALF, rows), F32)] * 2 + [pltpu.VMEM((RANK, rows), BF16)],
    )(me, *before, *parts, *buffer)


def solved(inverse, wide_ref, out_ref, pair_ref):
    inverse = split(inverse)
    square = jnp.zeros((HALF, 1), F32)
    step = 2 * TILE
    for c in range(wide_ref.shape[1] // step):
        lanes = pl.ds(step * c, step)
        part = dot3(inverse, split(wide_ref[:, lanes]))
        out_ref[:, lanes] = part
        pair_ref[:HALF, lanes], pair_ref[HALF:, lanes] = split(part)
        square = square + jnp.sum(part * part, axis=1, keepdims=True)
    return jnp.broadcast_to(square, (HALF, HALF)).T[:SUB, :]


def first_kernel(me_ref, mine_ref, other_ref, inverse_ref, wide_ref, out_ref, pair_ref, square_ref, gram_ref):
    me = me_ref[0]
    place(gram_ref, me, mine_ref[:, :HALF], other_ref[:, :HALF])
    place(wide_ref, me, mine_ref[:, HALF:], other_ref[:, HALF:])
    inverse_ref[...] = inverse_factor(gram_ref[...])
    square_ref[...] = solved(inverse_ref[...], wide_ref, out_ref, pair_ref)


def first_solve(me, mine, other):
    cols = mine.shape[1] - HALF
    return call(
        first_kernel, "first_solve", 5_000_000_000, 20 * HALF * cols,
        out_shape=[shaped(HALF, HALF), shaped(HALF, cols), shaped(HALF, cols), shaped(RANK, cols, dtype=BF16), shaped(SUB, HALF)],
        in_specs=[SMEM, VMEM, VMEM], out_specs=[VMEM] * 5, scratch_shapes=[pltpu.VMEM((HALF, HALF), F32)],
    )(me, mine, other)


def second_kernel(me_ref, mine_ref, other_ref, first_ref, wide0_ref, inverse_ref, out_ref, pair_ref, square_ref, gram_ref, wide_ref):
    me = me_ref[0]
    place(gram_ref, me, mine_ref[:, :RANK], other_ref[:, :RANK])
    place(wide_ref.at[HALF:, :], me, mine_ref[:, RANK:], other_ref[:, RANK:])
    wide_ref[:HALF, :] = wide0_ref[...]
    first = first_ref[...]
    side = dot(gram_ref[:, :HALF], first, NT, HIGHEST)
    second = inverse_factor(gram_ref[:, HALF:] - dot(side, side, NT, HIGHEST))
    inverse_ref[:HALF, :HALF] = first
    inverse_ref[:HALF, HALF:] = jnp.zeros((HALF, HALF), F32)
    inverse_ref[HALF:, :HALF] = -dot(second, dot(side, first, precision=HIGHEST), precision=HIGHEST)
    inverse_ref[HALF:, HALF:] = second
    square_ref[...] = solved(inverse_ref[HALF:, :], wide_ref, out_ref, pair_ref)


def second_solve(me, mine, other, first, wide0):
    cols = mine.shape[1] - RANK
    return call(
        second_kernel, "second_solve", 6_000_000_000, 20 * HALF * cols,
        out_shape=[shaped(RANK, RANK), shaped(HALF, cols), shaped(RANK, cols, dtype=BF16), shaped(SUB, HALF)],
        in_specs=[SMEM] + [VMEM] * 4, out_specs=[VMEM] * 4,
        scratch_shapes=[pltpu.VMEM((HALF, RANK), F32), pltpu.VMEM((RANK, cols), F32)],
    )(me, mine, other, first, wide0)


def ortho_kernel(left0_ref, left1_ref, inverse_ref, out_ref):
    left = jnp.concatenate([left0_ref[...], left1_ref[...]], axis=1)
    out_ref[...] = dot3(split(left), split(inverse_ref[...]), NT)


def ortho_product(left0, left1, inverse):
    rows = left0.shape[0]
    return call(
        ortho_kernel, "ortho", 6 * rows * RANK * RANK, 8 * rows * RANK,
        out_shape=shaped(rows, RANK), in_specs=[VMEM] * 3, out_specs=VMEM,
    )(left0, left1, inverse)


def update_kernel(ortho_ref, s0, s1, s2, s3, pair0_ref, pair1_ref, factor0_ref, factor1_ref, high_ref, low_ref, weight_ref, *refs):
    momentum_ref, out_ref, basis_ref, half_ref, triple_ref = refs
    total = (s0[0:1, :] + s1[0:1, :]) + (s2[0:1, :] + s3[0:1, :])
    scale = 1.0 / jnp.sqrt(total / F32(D) + F32(1e-06))
    step, width = pl.program_id(0), out_ref.shape[1]

    @pl.when(step == 0)
    def _():
        half_ref[...] = (F32(1.0 - beta_mom) * ortho_ref[...]).astype(BF16)
        high, low = split(ortho_ref[...] * (scale * F32(learn_rate * (D / RANK) ** 0.5)))
        triple_ref[:, :RANK] = high
        triple_ref[:, RANK:2 * RANK] = low
        triple_ref[:, 2 * RANK:] = high

    lanes = pl.ds(pl.multiple_of(step * width, width), width)
    high = [pair0_ref[:HALF, lanes], pair1_ref[:HALF, lanes]]
    feedback = dot(half_ref[...], jnp.concatenate(high, axis=0))
    momentum_ref[...] = (high_ref[:, lanes].astype(F32) + low_ref[:, lanes].astype(F32)) - feedback
    factor = jnp.concatenate([*high, *high, pair0_ref[HALF:, lanes], pair1_ref[HALF:, lanes]], axis=0)
    out_ref[...] = weight_ref[:, lanes] - dot(triple_ref[...], factor)
    basis_ref[:, :HALF] = factor0_ref[:, lanes].T * scale[:, :HALF]
    basis_ref[:, HALF:] = factor1_ref[:, lanes].T * scale[:, HALF:]


def update(ortho, squares, pairs, factors, buffer, weight):
    rows, cols = weight.shape
    tall = pl.BlockSpec((rows, TILE), lambda i: (0, i))
    return call(
        update_kernel, "update", 8 * rows * cols * RANK, 8 * rows * cols,
        out_shape=[shaped(rows, cols)] * 2 + [shaped(cols, RANK)], grid=(cols // TILE,), in_specs=[VMEM] * 12,
        out_specs=[tall, tall, pl.BlockSpec((TILE, RANK), lambda i: (i, 0))],
        scratch_shapes=[pltpu.VMEM((rows, RANK), BF16), pltpu.VMEM((rows, 3 * RANK), BF16)],
    )(ortho, *squares, *pairs, *factors, *buffer, weight)


def swap(x, axis, bit):
    size = lax.axis_size(axis)
    return lax.ppermute(x, axis, [(i, i ^ bit) for i in range(size)])


def together(*arrays):
    return lax.optimization_barrier(arrays)


def tuned(momentum, gradient, weight, right_basis):
    row = lax.axis_index("row")
    me = (2 * (row & 1) + ((row >> 1) & 1)).astype(jnp.int32)[None]
    high, low, up0, down0, second = start(me, momentum[0], gradient[0], right_basis)
    buffer = (high, low)
    got0 = swap(up0, "col", 1), swap(down0, "col", 2)
    up1, down1 = left_product(buffer, second, dims=NN)
    up0, down0, got0, up1, down1 = together(up0, down0, got0, up1, down1)
    for sweep in range(ITERS):
        last, scaled = sweep == ITERS - 1, sweep > 0

        up0, down0 = up0 + got0[0], down0 + got0[1]
        got0 = swap(up0, "col", 2), swap(down0, "col", 1)
        if sweep:
            up1, down1 = left_product(buffer, split1, square1)
        up0, down0, got0, up1, down1 = together(up0, down0, got0, up1, down1)

        keep0, give0, left0 = product(scaled, me, (), (up0, got0[0], down0, got0[1]), buffer)
        got1 = swap(up1, "col", 1), swap(down1, "col", 2)
        keep0, give0, left0, up1, down1, got1 = together(keep0, give0, left0, up1, down1, got1)

        part0 = keep0 + swap(give0, "row", 1)
        pair0 = swap(part0[PART:], "row", 2)
        up1, down1 = up1 + got1[0], down1 + got1[1]
        got1 = swap(up1, "col", 2), swap(down1, "col", 1)
        keep1, give1, left1 = product(scaled, me, (left0,), (up1, got1[0], down1, got1[1]), buffer)
        part0, pair0, keep1, give1 = together(part0, pair0, keep1, give1)

        core1 = swap(give1, "row", 1)
        part0, pair0, keep1, core1 = together(part0, pair0, keep1, core1)

        side0 = part0[:PART] + pair0
        cross0 = swap(side0, "row", 4)
        part1 = keep1 + core1
        pair1 = swap(part1[PART:], "row", 2)
        side0, cross0, part1, pair1 = together(side0, cross0, part1, pair1)

        total0 = side0 + cross0
        back0 = swap(total0, "row", 2)
        side1 = part1[:PART] + pair1
        cross1 = swap(side1, "row", 4)
        total0, back0, side1, cross1 = together(total0, back0, side1, cross1)

        mine0 = jnp.concatenate([total0, back0], axis=0)
        other0 = swap(mine0, "row", 1)
        total1 = side1 + cross1
        back1 = swap(total1, "row", 2)
        first, wide, factor0, split0, square0 = first_solve(me, mine0, other0)
        if not last:
            up0, down0 = left_product(buffer, split0, square0)
        total1, back1, first, wide, split0, square0, up0, down0 = together(total1, back1, first, wide, split0, square0, up0, down0)

        mine1 = jnp.concatenate([total1, back1], axis=0)
        other1 = swap(mine1, "row", 1)
        if not last:
            got0 = swap(up0, "col", 1), swap(down0, "col", 2)
        inverse, factor1, split1, square1 = second_solve(me, mine1, other1, first, wide)
        if not last:
            up0, down0, got0, split1, square1 = together(up0, down0, got0, split1, square1)

    square = jnp.concatenate([square0, square1], axis=1)
    squares = (square, swap(square, "col", 1), swap(square, "col", 2), swap(square, "col", 3))
    ortho = ortho_product(left0, left1, inverse)
    squares = together(*squares, ortho)[:4]
    new_momentum, new_weight, new_basis = update(ortho, squares, (split0, split1), (factor0, factor1), buffer, weight)
    return new_momentum[None], new_weight, new_basis


def general(momentum, gradient, weight, right_basis):
    replicas = lax.axis_size("rep")
    buffer = momentum[0] + gradient[0].astype(F32)
    basis, dims = right_basis, NN
    for sweep in range(ITERS):
        left = lax.psum(dot(buffer, basis, dims, HIGH) / replicas, ("col", "rep"))
        if sweep:
            left = left / rms
        gram = lax.psum(dot(left, left, ((0,), (0,)), HIGHEST), "row")
        wide = lax.psum(dot(left, buffer, ((0,), (0,)), HIGH) / replicas, ("row", "rep"))
        inverse = inverse_cholesky(gram)
        factor = dot(inverse, wide, precision=HIGHEST)
        rms = jnp.sqrt(lax.psum(jnp.sum(factor * factor, axis=1)[None, :], "col") / F32(D) + 1e-06)
        basis, dims = factor, NT
    ortho = dot(left, inverse, NT, HIGHEST)
    new_momentum = (buffer - (1.0 - beta_mom) * dot(ortho, factor, precision=HIGH))[None]
    basis = factor / rms.T
    new_weight = weight - learn_rate * jnp.sqrt(F32(D) / F32(RANK)) * dot(ortho, basis, precision=HIGH)
    return new_momentum, new_weight, basis.T


def solution(mesh):
    sizes = dict(mesh.shape)
    fits = sizes["row"] == 8 and sizes["col"] == 4 and sizes["rep"] == 1
    return jax.shard_map(
        tuned if fits else general,
        mesh=mesh,
        in_specs=(P("rep", "row", "col"), P("rep", "row", "col"), P("row", "col"), P("col", None)),
        out_specs=(P("rep", "row", "col"), P("row", "col"), P("col", None)),
        check_vma=False,
    )
```

profile of v0, /device:TPU:0, one launch (start us, length us, event | category | flops | bytes accessed | tf_op | source)
XLA Modules:
  0.0 193.8 jit_solution(11595613347796646281)
XLA Ops:
  0.6 7.0 %start.1 = (bf16[1024,2048]{1,0:T(8,128)(2,1)S(1)}, bf16[1024,2048]{1,0:T(8,128)(2,1)S(1)}, f32[512,128]{1,0:T(8,128)S(1)}, f32[512,128]{1,0:T(8,128)S(1)}, bf16[2048,256]{1,0:T(8,128)(2,1)S(1)}) custom-call(s32[1]{0:T(128)} %bitcast.me_ref, f32[1024,2048]{1,0:T(8,128)} %bitcast.6, bf16[1024,2048]{1,0:T(8,128)(2,1)} %bitcast.7, f32[2048,256]{1,0:T(8,128)} %basis_ref.1), custom_call_target="tpu_custom_call" | custom-call | flops 2147483648 | bytes 12582912 | tf_op jit(solution)/shard_map/start/pallas_call | solution.py:164
  7.7 3.0 %collective-permute-start = (f32[512,128]{1,0:T(8,128)S(1)}, f32[512,128]{1,0:T(8,128)S(1)}, u32[]{:S(2)}, u32[]{:S(2)}) collective-permute-start(f32[512,128]{1,0:T(8,128)S(1)} %get-tuple-element.136), channel_id=1, source_target_pairs={{0,1},{1,0},{2,3},{3,2},{4,5},{5,4},{6,7},{7,6},{8,9},{9,8},{10,11... | collective-permute-start | bytes 786440 | tf_op jit(solution)/shard_map/ppermute | solution.py:354
  12.2 2.9 %left.3 = (f32[512,128]{1,0:T(8,128)S(1)}, f32[512,128]{1,0:T(8,128)S(1)}) custom-call(bf16[1024,2048]{1,0:T(8,128)(2,1)S(1)} %get-tuple-element.131.high_ref.refs_4_.refs_5_, bf16[1024,2048]{1,0:T(8,128)(2,1)S(1)} %get-tuple-element.132.low_ref.refs_5_.refs_6_, bf16[2048,256]{1,0:T(8,128)(2,1)S(1)} %get-tuple-element.133.factor_ref), custom_call_target="tpu_custom_call" | custom-call | bytes 8388608 | tf_op jit(solution)/shard_map/left/pallas_call | solution.py:197
  20.7 4.7 %collective-permute-done.3.refs_3_ = f32[512,128]{1,0:T(8,128)S(1)} collective-permute-done((f32[512,128]{1,0:T(8,128)S(1)}, f32[512,128]{1,0:T(8,128)S(1)}, u32[]{:S(2)}, u32[]{:S(2)}) %collective-permute-start.3) | collective-permute-done | bytes 262176 | tf_op jit(solution)/shard_map/ppermute | solution.py:354
  37.7 4.8 %collective-permute-done.9.refs_4_ = f32[512,128]{1,0:T(8,128)S(1)} collective-permute-done((f32[512,128]{1,0:T(8,128)S(1)}, f32[512,128]{1,0:T(8,128)S(1)}, u32[]{:S(2)}, u32[]{:S(2)}) %collective-permute-start.9) | collective-permute-done | bytes 262176 | tf_op jit(solution)/shard_map/ppermute | solution.py:354
  42.9 3.5 %product.5 = (f32[64,2304]{1,0:T(8,128)S(1)}, f32[64,2304]{1,0:T(8,128)S(1)}, f32[1024,128]{1,0:T(8,128)}) custom-call(s32[1]{0:T(128)} %bitcast.me_ref, f32[1024,128]{1,0:T(8,128)S(1)} %get-tuple-element.153.refs_0_, f32[512,128]{1,0:T(8,128)S(1)} %add.67.refs_1_, f32[512,128]{1,0:T(8,128)S(1)} %collective-permute-done.8.refs_2_, ...), custom_call_target="tpu_custom_call" | custom-call | flops 2415919104 | bytes 9437184 | tf_op jit(solution)/shard_map/product/pallas_call | solution.py:241
  50.1 2.7 %collective-permute-start.11 = (f32[32,2176]{1,0:T(8,128)S(1)}, f32[32,2176]{1,0:T(8,128)S(1)}, u32[]{:S(2)}, u32[]{:S(2)}) collective-permute-start(f32[32,2176]{1,0:T(8,128)S(1)} %slice_add_fusion.3), channel_id=1, source_target_pairs={{0,16},{4,20},{8,24},{12,28},{16,0},{20,4},{24,8},{28,12},{1,17},{... | collective-permute-start | bytes 835592 | tf_op jit(solution)/shard_map/ppermute | solution.py:354
  52.7 9.9 %collective-permute-done.11 = f32[32,2176]{1,0:T(8,128)S(1)} collective-permute-done((f32[32,2176]{1,0:T(8,128)S(1)}, f32[32,2176]{1,0:T(8,128)S(1)}, u32[]{:S(2)}, u32[]{:S(2)}) %collective-permute-start.11) | collective-permute-done | bytes 278560 | tf_op jit(solution)/shard_map/ppermute | solution.py:354
  63.6 2.6 %collective-permute-start.14 = (f32[32,2304]{1,0:T(8,128)S(1)}, f32[32,2304]{1,0:T(8,128)S(1)}, u32[]{:S(2)}, u32[]{:S(2)}) collective-permute-start(f32[32,2304]{1,0:T(8,128)S(1)} %slice_add_fusion.1), channel_id=1, source_target_pairs={{0,16},{4,20},{8,24},{12,28},{16,0},{20,4},{24,8},{28,12},{1,17},{... | collective-permute-start | bytes 884744 | tf_op jit(solution)/shard_map/ppermute | solution.py:354
  68.7 9.2 %collective-permute-done.13 = f32[32,2176]{1,0:T(8,128)S(1)} collective-permute-done((f32[32,2176]{1,0:T(8,128)S(1)}, f32[32,2176]{1,0:T(8,128)S(1)}, u32[]{:S(2)}, u32[]{:S(2)}) %collective-permute-start.13) | collective-permute-done | bytes 278560 | tf_op jit(solution)/shard_map/ppermute | solution.py:354
  81.2 5.6 %first_solve.2 = (f32[128,128]{1,0:T(8,128)S(1)}, f32[128,2048]{1,0:T(8,128)S(1)}, f32[128,2048]{1,0:T(8,128)}, bf16[256,2048]{1,0:T(8,128)(2,1)S(1)}, f32[8,128]{1,0:T(8,128)S(1)}) custom-call(s32[1]{0:T(128)} %bitcast.me_ref, f32[64,2176]{1,0:T(8,128)S(1)} %constant_dynamic-update-slice_fusion.mine_ref, f32[64,2176]{1,0:T(8,128)S(1)} %collective-permute-done.16.other_ref), custom_call_target="tpu_custom_call" | custom-call | flops 5000000000 | bytes 5242880 | tf_op jit(solution)/shard_map/first_solve/pallas_call | solution.py:272
  86.8 3.0 %left.4 = (f32[520,128]{1,0:T(8,128)S(1)}, f32[512,128]{1,0:T(8,128)S(1)}) custom-call(bf16[1024,2048]{1,0:T(8,128)(2,1)S(1)} %get-tuple-element.131.high_ref.refs_4_.refs_5_, bf16[1024,2048]{1,0:T(8,128)(2,1)S(1)} %get-tuple-element.132.low_ref.refs_5_.refs_6_, bf16[256,2048]{1,0:T(8,128)(2,1)S(1)} %get-tuple-element.178.factor_ref, ...), custom_call_target="tpu_custom_call" | custom-call | bytes 8388608 | tf_op jit(solution)/shard_map/left/pallas_call | solution.py:197
  93.0 6.6 %second_solve.2 = (f32[256,256]{1,0:T(8,128)}, f32[128,2048]{1,0:T(8,128)}, bf16[256,2048]{1,0:T(8,128)(2,1)S(1)}, f32[8,128]{1,0:T(8,128)S(1)}) custom-call(s32[1]{0:T(128)} %bitcast.me_ref, f32[64,2304]{1,0:T(8,128)S(1)} %constant_dynamic-update-slice_fusion.2.mine_ref, f32[64,2304]{1,0:T(8,128)S(1)} %collective-permute-done.19.other_ref, ...), custom_call_target="tpu_custom_call" | custom-call | flops 6000000000 | bytes 5242880 | tf_op jit(solution)/shard_map/second_solve/pallas_call | solution.py:296
  102.0 3.0 %left.5 = (f32[520,128]{1,0:T(8,128)S(1)}, f32[512,128]{1,0:T(8,128)S(1)}) custom-call(bf16[1024,2048]{1,0:T(8,128)(2,1)S(1)} %get-tuple-element.131.high_ref.refs_4_.refs_5_, bf16[1024,2048]{1,0:T(8,128)(2,1)S(1)} %get-tuple-element.132.low_ref.refs_5_.refs_6_, bf16[256,2048]{1,0:T(8,128)(2,1)S(1)} %get-tuple-element.194.factor_ref, ...), custom_call_target="tpu_custom_call" | custom-call | bytes 8388608 | tf_op jit(solution)/shard_map/left/pallas_call | solution.py:197
  105.0 3.2 %collective-permute-done.21.refs_3_ = f32[512,128]{1,0:T(8,128)S(1)} collective-permute-done((f32[512,128]{1,0:T(8,128)S(1)}, f32[512,128]{1,0:T(8,128)S(1)}, u32[]{:S(2)}, u32[]{:S(2)}) %collective-permute-start.21) | collective-permute-done | bytes 262176 | tf_op jit(solution)/shard_map/ppermute | solution.py:354
  113.2 2.9 %collective-permute-done.23 = f32[512,128]{1,0:T(8,128)S(1)} collective-permute-done((f32[512,128]{1,0:T(8,128)S(1)}, f32[512,128]{1,0:T(8,128)S(1)}, u32[]{:S(2)}, u32[]{:S(2)}) %collective-permute-start.23) | collective-permute-done | bytes 262176 | tf_op jit(solution)/shard_map/ppermute | solution.py:354
  119.6 6.1 %collective-permute-done.25.refs_4_ = f32[512,128]{1,0:T(8,128)S(1)} collective-permute-done((f32[512,128]{1,0:T(8,128)S(1)}, f32[512,128]{1,0:T(8,128)S(1)}, u32[]{:S(2)}, u32[]{:S(2)}) %collective-permute-start.25) | collective-permute-done | bytes 262176 | tf_op jit(solution)/shard_map/ppermute | solution.py:354
  125.7 2.9 %product.7 = (f32[64,2304]{1,0:T(8,128)S(1)}, f32[64,2304]{1,0:T(8,128)S(1)}, f32[1024,128]{1,0:T(8,128)S(1)}) custom-call(s32[1]{0:T(128)} %bitcast.me_ref, f32[1024,128]{1,0:T(8,128)S(1)} %get-tuple-element.207.refs_0_.left0_ref, f32[520,128]{1,0:T(8,128)S(1)} %add.76.refs_1_, f32[520,128]{1,0:T(8,128)S(1)} %collective-permute-done.24.refs_2_, ...), custom_call_target="tpu_custom_call" | custom-call | flops 2415919104 | bytes 9437184 | tf_op jit(solution)/shard_map/product/pallas_call | solution.py:241
  134.1 10.6 %collective-permute-done.29 = f32[32,2176]{1,0:T(8,128)S(1)} collective-permute-done((f32[32,2176]{1,0:T(8,128)S(1)}, f32[32,2176]{1,0:T(8,128)S(1)}, u32[]{:S(2)}, u32[]{:S(2)}) %collective-permute-start.29) | collective-permute-done | bytes 278560 | tf_op jit(solution)/shard_map/ppermute | solution.py:354
  150.8 9.2 %collective-permute-done.31 = f32[32,2176]{1,0:T(8,128)S(1)} collective-permute-done((f32[32,2176]{1,0:T(8,128)S(1)}, f32[32,2176]{1,0:T(8,128)S(1)}, u32[]{:S(2)}, u32[]{:S(2)}) %collective-permute-start.31) | collective-permute-done | bytes 278560 | tf_op jit(solution)/shard_map/ppermute | solution.py:354
  163.5 4.8 %first_solve.3 = (f32[128,128]{1,0:T(8,128)S(1)}, f32[128,2048]{1,0:T(8,128)S(1)}, f32[128,2048]{1,0:T(8,128)S(1)}, bf16[256,2048]{1,0:T(8,128)(2,1)S(1)}, f32[8,128]{1,0:T(8,128)S(1)}) custom-call(s32[1]{0:T(128)} %bitcast.me_ref, f32[64,2176]{1,0:T(8,128)S(1)} %constant_dynamic-update-slice_fusion.4.mine_ref, f32[64,2176]{1,0:T(8,128)S(1)} %collective-permute-done.34.other_ref), custom_call_target="tpu_custom_call" | custom-call | flops 5000000000 | bytes 5242880 | tf_op jit(solution)/shard_map/first_solve/pallas_call | solution.py:272
  168.3 2.8 %collective-permute-done.33 = f32[32,2304]{1,0:T(8,128)S(1)} collective-permute-done((f32[32,2304]{1,0:T(8,128)S(1)}, f32[32,2304]{1,0:T(8,128)S(1)}, u32[]{:S(2)}, u32[]{:S(2)}) %collective-permute-start.33) | collective-permute-done | bytes 294944 | tf_op jit(solution)/shard_map/ppermute | solution.py:354
  173.2 5.9 %second_solve.3 = (f32[256,256]{1,0:T(8,128)S(1)}, f32[128,2048]{1,0:T(8,128)S(1)}, bf16[256,2048]{1,0:T(8,128)(2,1)S(1)}, f32[8,128]{1,0:T(8,128)S(1)}) custom-call(s32[1]{0:T(128)} %bitcast.me_ref, f32[64,2304]{1,0:T(8,128)S(1)} %constant_dynamic-update-slice_fusion.6.mine_ref, f32[64,2304]{1,0:T(8,128)S(1)} %collective-permute-done.35.other_ref, ...), custom_call_target="tpu_custom_call" | custom-call | flops 6000000000 | bytes 5242880 | tf_op jit(solution)/shard_map/second_solve/pallas_call | solution.py:296
  185.1 8.8 %update.1 = (f32[1024,2048]{1,0:T(8,128)}, f32[1024,2048]{1,0:T(8,128)}, f32[2048,256]{1,0:T(8,128)}) custom-call(f32[1024,256]{1,0:T(8,128)S(1)} %ortho.1.ortho_ref, f32[8,256]{1,0:T(8,128)S(1)} %constant_dynamic-update-slice_fusion.8.s0, f32[8,256]{1,0:T(8,128)S(1)} %collective-permute-done.36.s1, f32[8,256]{1,0:T(8,128)S(1)} %collective-permute-done.37.s2, ...), custom_call_target="tpu_custom_call" | custom-call | flops 4294967296 | bytes 16777216 | tf_op jit(solution)/shard_map/update/pallas_call | solution.py:344
  (107 shorter events, 67.4 us)
Async XLA Ops:
  7.7 9.3 %collective-permute-start = (f32[512,128]{1,0:T(8,128)S(1)}, f32[512,128]{1,0:T(8,128)S(1)}, u32[]{:S(2)}, u32[]{:S(2)}) collective-permute-start(f32[512,128]{1,0:T(8,128)S(1)} %get-tuple-element.136), channel_id=1, source_target_pairs={{0,1},{1,0},{2,3},{3,2},{4,5},{5,4},{6,7},{7,6},{8,9},{9,8},{10,11... | collective-permute-start | bytes 786440 | tf_op jit(solution)/shard_map/ppermute | solution.py:354
  10.7 7.8 %collective-permute-start.1 = (f32[512,128]{1,0:T(8,128)S(1)}, f32[512,128]{1,0:T(8,128)S(1)}, u32[]{:S(2)}, u32[]{:S(2)}) collective-permute-start(f32[512,128]{1,0:T(8,128)S(1)} %get-tuple-element.138), channel_id=1, source_target_pairs={{0,2},{1,3},{2,0},{3,1},{4,6},{5,7},{6,4},{7,5},{8,10},{9,11},{10,... | collective-permute-start | bytes 786440 | tf_op jit(solution)/shard_map/ppermute | solution.py:354
  18.9 7.0 %collective-permute-start.2 = (f32[512,128]{1,0:T(8,128)S(1)}, f32[512,128]{1,0:T(8,128)S(1)}, u32[]{:S(2)}, u32[]{:S(2)}) collective-permute-start(f32[512,128]{1,0:T(8,128)S(1)} %add.64.refs_0_), channel_id=1, source_target_pairs={{0,2},{1,3},{2,0},{3,1},{4,6},{5,7},{6,4},{7,5},{8,10},{9,11},{10,... | collective-permute-start | bytes 786440 | tf_op jit(solution)/shard_map/ppermute | solution.py:354
  33.6 8.8 %collective-permute-start.9 = (f32[512,128]{1,0:T(8,128)S(1)}, f32[512,128]{1,0:T(8,128)S(1)}, u32[]{:S(2)}, u32[]{:S(2)}) collective-permute-start(f32[512,128]{1,0:T(8,128)S(1)} %add.68.refs_3_), channel_id=1, source_target_pairs={{0,1},{1,0},{2,3},{3,2},{4,5},{5,4},{6,7},{7,6},{8,9},{9,8},{10,11... | collective-permute-start | bytes 786440 | tf_op jit(solution)/shard_map/ppermute | solution.py:354
  34.4 8.5 %collective-permute-start.8 = (f32[512,128]{1,0:T(8,128)S(1)}, f32[512,128]{1,0:T(8,128)S(1)}, u32[]{:S(2)}, u32[]{:S(2)}) collective-permute-start(f32[512,128]{1,0:T(8,128)S(1)} %add.67.refs_1_), channel_id=1, source_target_pairs={{0,2},{1,3},{2,0},{3,1},{4,6},{5,7},{6,4},{7,5},{8,10},{9,11},{10,... | collective-permute-start | bytes 786440 | tf_op jit(solution)/shard_map/ppermute | solution.py:354
  36.0 10.4 %collective-permute-start.7 = (f32[32,2176]{1,0:T(8,128)S(1)}, f32[32,2176]{1,0:T(8,128)S(1)}, u32[]{:S(2)}, u32[]{:S(2)}) collective-permute-start(f32[32,2176]{1,0:T(8,128)S(1)} %slice.32), channel_id=1, source_target_pairs={{0,8},{4,12},{8,0},{12,4},{16,24},{20,28},{24,16},{28,20},{1,9},{5... | collective-permute-start | bytes 835592 | tf_op jit(solution)/shard_map/ppermute | solution.py:354
  48.5 15.1 %collective-permute-start.12 = (f32[32,2304]{1,0:T(8,128)S(1)}, f32[32,2304]{1,0:T(8,128)S(1)}, u32[]{:S(2)}, u32[]{:S(2)}) collective-permute-start(f32[32,2304]{1,0:T(8,128)S(1)} %slice.33), channel_id=1, source_target_pairs={{0,8},{4,12},{8,0},{12,4},{16,24},{20,28},{24,16},{28,20},{1,9},{5... | collective-permute-start | bytes 884744 | tf_op jit(solution)/shard_map/ppermute | solution.py:354
  50.1 12.6 %collective-permute-start.11 = (f32[32,2176]{1,0:T(8,128)S(1)}, f32[32,2176]{1,0:T(8,128)S(1)}, u32[]{:S(2)}, u32[]{:S(2)}) collective-permute-start(f32[32,2176]{1,0:T(8,128)S(1)} %slice_add_fusion.3), channel_id=1, source_target_pairs={{0,16},{4,20},{8,24},{12,28},{16,0},{20,4},{24,8},{28,12},{1,17},{... | collective-permute-start | bytes 835592 | tf_op jit(solution)/shard_map/ppermute | solution.py:354
  63.6 15.5 %collective-permute-start.14 = (f32[32,2304]{1,0:T(8,128)S(1)}, f32[32,2304]{1,0:T(8,128)S(1)}, u32[]{:S(2)}, u32[]{:S(2)}) collective-permute-start(f32[32,2304]{1,0:T(8,128)S(1)} %slice_add_fusion.1), channel_id=1, source_target_pairs={{0,16},{4,20},{8,24},{12,28},{16,0},{20,4},{24,8},{28,12},{1,17},{... | collective-permute-start | bytes 884744 | tf_op jit(solution)/shard_map/ppermute | solution.py:354
  66.2 11.7 %collective-permute-start.13 = (f32[32,2176]{1,0:T(8,128)S(1)}, f32[32,2176]{1,0:T(8,128)S(1)}, u32[]{:S(2)}, u32[]{:S(2)}) collective-permute-start(f32[32,2176]{1,0:T(8,128)S(1)} %add.71), channel_id=1, source_target_pairs={{0,8},{4,12},{8,0},{12,4},{16,24},{20,28},{24,16},{28,20},{1,9},{5... | collective-permute-start | bytes 835592 | tf_op jit(solution)/shard_map/ppermute | solution.py:354
  79.3 10.5 %collective-permute-start.15 = (f32[32,2304]{1,0:T(8,128)S(1)}, f32[32,2304]{1,0:T(8,128)S(1)}, u32[]{:S(2)}, u32[]{:S(2)}) collective-permute-start(f32[32,2304]{1,0:T(8,128)S(1)} %add.73), channel_id=1, source_target_pairs={{0,8},{4,12},{8,0},{12,4},{16,24},{20,28},{24,16},{28,20},{1,9},{5... | collective-permute-start | bytes 884744 | tf_op jit(solution)/shard_map/ppermute | solution.py:354
  90.1 9.5 %collective-permute-start.18 = (f32[512,128]{1,0:T(8,128)S(1)}, f32[512,128]{1,0:T(8,128)S(1)}, u32[]{:S(2)}, u32[]{:S(2)}) collective-permute-start(f32[512,128]{1,0:T(8,128)S(1)} %get-tuple-element.192), channel_id=1, source_target_pairs={{0,2},{1,3},{2,0},{3,1},{4,6},{5,7},{6,4},{7,5},{8,10},{9,11},{10,... | collective-permute-start | bytes 786440 | tf_op jit(solution)/shard_map/ppermute | solution.py:354
  91.5 8.4 %collective-permute-start.17 = (f32[520,128]{1,0:T(8,128)S(1)}, f32[520,128]{1,0:T(8,128)S(1)}, u32[]{:S(2)}, u32[]{:S(2)}) collective-permute-start(f32[520,128]{1,0:T(8,128)S(1)} %get-tuple-element.190), channel_id=1, source_target_pairs={{0,1},{1,0},{2,3},{3,2},{4,5},{5,4},{6,7},{7,6},{8,9},{9,8},{10,11... | collective-permute-start | bytes 798728 | tf_op jit(solution)/shard_map/ppermute | solution.py:354
  100.0 8.3 %collective-permute-start.20 = (f32[520,128]{1,0:T(8,128)S(1)}, f32[520,128]{1,0:T(8,128)S(1)}, u32[]{:S(2)}, u32[]{:S(2)}) collective-permute-start(f32[520,128]{1,0:T(8,128)S(1)} %add.74.refs_0_), channel_id=1, source_target_pairs={{0,2},{1,3},{2,0},{3,1},{4,6},{5,7},{6,4},{7,5},{8,10},{9,11},{10,... | collective-permute-start | bytes 798728 | tf_op jit(solution)/shard_map/ppermute | solution.py:354
  100.6 7.6 %collective-permute-start.21 = (f32[512,128]{1,0:T(8,128)S(1)}, f32[512,128]{1,0:T(8,128)S(1)}, u32[]{:S(2)}, u32[]{:S(2)}) collective-permute-start(f32[512,128]{1,0:T(8,128)S(1)} %add.75.refs_2_), channel_id=1, source_target_pairs={{0,1},{1,0},{2,3},{3,2},{4,5},{5,4},{6,7},{7,6},{8,9},{9,8},{10,11... | collective-permute-start | bytes 786440 | tf_op jit(solution)/shard_map/ppermute | solution.py:354
  108.3 7.8 %collective-permute-start.22 = (f32[520,128]{1,0:T(8,128)S(1)}, f32[520,128]{1,0:T(8,128)S(1)}, u32[]{:S(2)}, u32[]{:S(2)}) collective-permute-start(f32[520,128]{1,0:T(8,128)S(1)} %get-tuple-element.208), channel_id=1, source_target_pairs={{0,1},{1,0},{2,3},{3,2},{4,5},{5,4},{6,7},{7,6},{8,9},{9,8},{10,11... | collective-permute-start | bytes 798728 | tf_op jit(solution)/shard_map/ppermute | solution.py:354
  116.2 9.6 %collective-permute-start.24 = (f32[520,128]{1,0:T(8,128)S(1)}, f32[520,128]{1,0:T(8,128)S(1)}, u32[]{:S(2)}, u32[]{:S(2)}) collective-permute-start(f32[520,128]{1,0:T(8,128)S(1)} %add.76.refs_1_), channel_id=1, source_target_pairs={{0,2},{1,3},{2,0},{3,1},{4,6},{5,7},{6,4},{7,5},{8,10},{9,11},{10,... | collective-permute-start | bytes 798728 | tf_op jit(solution)/shard_map/ppermute | solution.py:354
  117.2 8.5 %collective-permute-start.25 = (f32[512,128]{1,0:T(8,128)S(1)}, f32[512,128]{1,0:T(8,128)S(1)}, u32[]{:S(2)}, u32[]{:S(2)}) collective-permute-start(f32[512,128]{1,0:T(8,128)S(1)} %add.77.refs_3_), channel_id=1, source_target_pairs={{0,1},{1,0},{2,3},{3,2},{4,5},{5,4},{6,7},{7,6},{8,9},{9,8},{10,11... | collective-permute-start | bytes 786440 | tf_op jit(solution)/shard_map/ppermute | solution.py:354
  118.2 10.4 %collective-permute-start.27 = (f32[32,2176]{1,0:T(8,128)S(1)}, f32[32,2176]{1,0:T(8,128)S(1)}, u32[]{:S(2)}, u32[]{:S(2)}) collective-permute-start(f32[32,2176]{1,0:T(8,128)S(1)} %slice.34), channel_id=1, source_target_pairs={{0,8},{4,12},{8,0},{12,4},{16,24},{20,28},{24,16},{28,20},{1,9},{5... | collective-permute-start | bytes 835592 | tf_op jit(solution)/shard_map/ppermute | solution.py:354
  130.8 15.1 %collective-permute-start.30 = (f32[32,2304]{1,0:T(8,128)S(1)}, f32[32,2304]{1,0:T(8,128)S(1)}, u32[]{:S(2)}, u32[]{:S(2)}) collective-permute-start(f32[32,2304]{1,0:T(8,128)S(1)} %slice.35), channel_id=1, source_target_pairs={{0,8},{4,12},{8,0},{12,4},{16,24},{20,28},{24,16},{28,20},{1,9},{5... | collective-permute-start | bytes 884744 | tf_op jit(solution)/shard_map/ppermute | solution.py:354
  132.2 12.6 %collective-permute-start.29 = (f32[32,2176]{1,0:T(8,128)S(1)}, f32[32,2176]{1,0:T(8,128)S(1)}, u32[]{:S(2)}, u32[]{:S(2)}) collective-permute-start(f32[32,2176]{1,0:T(8,128)S(1)} %slice_add_fusion.2), channel_id=1, source_target_pairs={{0,16},{4,20},{8,24},{12,28},{16,0},{20,4},{24,8},{28,12},{1,17},{... | collective-permute-start | bytes 835592 | tf_op jit(solution)/shard_map/ppermute | solution.py:354
  145.9 15.5 %collective-permute-start.32 = (f32[32,2304]{1,0:T(8,128)S(1)}, f32[32,2304]{1,0:T(8,128)S(1)}, u32[]{:S(2)}, u32[]{:S(2)}) collective-permute-start(f32[32,2304]{1,0:T(8,128)S(1)} %slice_add_fusion), channel_id=1, source_target_pairs={{0,16},{4,20},{8,24},{12,28},{16,0},{20,4},{24,8},{28,12},{1,17},{... | collective-permute-start | bytes 884744 | tf_op jit(solution)/shard_map/ppermute | solution.py:354
  148.4 11.7 %collective-permute-start.31 = (f32[32,2176]{1,0:T(8,128)S(1)}, f32[32,2176]{1,0:T(8,128)S(1)}, u32[]{:S(2)}, u32[]{:S(2)}) collective-permute-start(f32[32,2176]{1,0:T(8,128)S(1)} %add.81), channel_id=1, source_target_pairs={{0,8},{4,12},{8,0},{12,4},{16,24},{20,28},{24,16},{28,20},{1,9},{5... | collective-permute-start | bytes 835592 | tf_op jit(solution)/shard_map/ppermute | solution.py:354
  161.6 9.5 %collective-permute-start.33 = (f32[32,2304]{1,0:T(8,128)S(1)}, f32[32,2304]{1,0:T(8,128)S(1)}, u32[]{:S(2)}, u32[]{:S(2)}) collective-permute-start(f32[32,2304]{1,0:T(8,128)S(1)} %add.83), channel_id=1, source_target_pairs={{0,8},{4,12},{8,0},{12,4},{16,24},{20,28},{24,16},{28,20},{1,9},{5... | collective-permute-start | bytes 884744 | tf_op jit(solution)/shard_map/ppermute | solution.py:354
  (17 other events, 83.3 us)
where the time goes:
time: 194 us
  waiting for transfers between devices  84.2 us (43%)
  Pallas kernels  59.3 us (31%)
  starting transfers between devices  48.3 us (25%)
    ppermute x39, waiting for transfers between devices, swap(): return lax.ppermute(x, axis, [(i, i ^ bit) for i in range(size)])  84.2 us
    ppermute x39, starting transfers between devices, swap(): return lax.ppermute(x, axis, [(i, i ^ bit) for i in range(size)])  48.3 us
    pallas_call x2, Pallas kernels, second_solve(): call(second_kernel, 'second_solve', 6000000000, 20 * HALF * cols, out_sha...  12.5 us
    pallas_call x4, Pallas kernels, product(): call(functools.partial(product_kernel, not before, scaled), 'product', 4...  11.2 us
    pallas_call x2, Pallas kernels, first_solve(): call(first_kernel, 'first_solve', 5000000000, 20 * HALF * cols, out_shape...  10.4 us
    pallas_call x3, Pallas kernels, left_product(): call(functools.partial(left_kernel, dims), 'left', 0, 4 * rows * cols, ou...  8.86 us
    pallas_call x1, Pallas kernels, update(): call(update_kernel, 'update', 8 * rows * cols * RANK, 8 * rows * cols, ou...  8.77 us
    pallas_call x1, Pallas kernels, start(): call(start_kernel, 'start', 4 * rows * cols * RANK, 6 * rows * cols, out_...  7.03 us
  transfers between devices with their start and end apart: 39, of which 29 were waited for; matrix products, arithmetic and copies ran while one was open for 0% of the time, Pallas kernels for 19%

commit v1 on v0

--- a/solution.py
+++ b/solution.py
@@ -314,9 +314,9 @@
     )(left0, left1, inverse)
 
 
-def update_kernel(ortho_ref, s0, s1, s2, s3, pair0_ref, pair1_ref, factor0_ref, factor1_ref, high_ref, low_ref, weight_ref, *refs):
+def update_kernel(ortho_ref, s0, s1, pair0_ref, pair1_ref, factor0_ref, factor1_ref, high_ref, low_ref, weight_ref, *refs):
     momentum_ref, out_ref, basis_ref, half_ref, triple_ref = refs
-    total = (s0[0:1, :] + s1[0:1, :]) + (s2[0:1, :] + s3[0:1, :])
+    total = s0[0:1, :] + s1[0:1, :]
     scale = 1.0 / jnp.sqrt(total / F32(D) + F32(1e-06))
     step, width = pl.program_id(0), out_ref.shape[1]
 
@@ -343,7 +343,7 @@
     tall = pl.BlockSpec((rows, TILE), lambda i: (0, i))
     return call(
         update_kernel, "update", 8 * rows * cols * RANK, 8 * rows * cols,
-        out_shape=[shaped(rows, cols)] * 2 + [shaped(cols, RANK)], grid=(cols // TILE,), in_specs=[VMEM] * 12,
+        out_shape=[shaped(rows, cols)] * 2 + [shaped(cols, RANK)], grid=(cols // TILE,), in_specs=[VMEM] * 10,
         out_specs=[tall, tall, pl.BlockSpec((TILE, RANK), lambda i: (i, 0))],
         scratch_shapes=[pltpu.VMEM((rows, RANK), BF16), pltpu.VMEM((rows, 3 * RANK), BF16)],
     )(ortho, *squares, *pairs, *factors, *buffer, weight)
@@ -386,18 +386,15 @@
         keep1, give1, left1 = product(scaled, me, (left0,), (up1, got1[0], down1, got1[1]), buffer)
         part0, pair0, keep1, give1 = together(part0, pair0, keep1, give1)
 
-        core1 = swap(give1, "row", 1)
-        part0, pair0, keep1, core1 = together(part0, pair0, keep1, core1)
-
         side0 = part0[:PART] + pair0
         cross0 = swap(side0, "row", 4)
-        part1 = keep1 + core1
-        pair1 = swap(part1[PART:], "row", 2)
+        part1 = keep1 + swap(give1, "row", 1)
+        pair1 = [swap(part1[rows], "row", 2) for rows in (slice(PART, PART + PART // 2), slice(PART + PART // 2, None))]
         side0, cross0, part1, pair1 = together(side0, cross0, part1, pair1)
 
         total0 = side0 + cross0
         back0 = swap(total0, "row", 2)
-        side1 = part1[:PART] + pair1
+        side1 = part1[:PART] + jnp.concatenate(pair1, axis=0)
         cross1 = swap(side1, "row", 4)
         total0, back0, side1, cross1 = together(total0, back0, side1, cross1)
 
@@ -419,10 +416,11 @@
             up0, down0, got0, split1, square1 = together(up0, down0, got0, split1, square1)
 
     square = jnp.concatenate([square0, square1], axis=1)
-    squares = (square, swap(square, "col", 1), swap(square, "col", 2), swap(square, "col", 3))
+    other = swap(square, "col", 1)
     ortho = ortho_product(left0, left1, inverse)
-    squares = together(*squares, ortho)[:4]
-    new_momentum, new_weight, new_basis = update(ortho, squares, (split0, split1), (factor0, factor1), buffer, weight)
+    square, other, ortho = together(square, other, ortho)
+    square = square + other
+    new_momentum, new_weight, new_basis = update(ortho, (square, swap(square, "col", 2)), (split0, split1), (factor0, factor1), buffer, weight)
     return new_momentum[None], new_weight, new_basis
 
 

time: 194 us -> 195 us (level)
  waiting for transfers between devices: 84.2 us -> 91.3 us
  starting transfers between devices: 48.3 us -> 42.2 us
    ppermute x39 -> x40, waiting for transfers between devices: 84.2 us -> 91.3 us  [swap(): return lax.ppermute(x, axis, [(i, i ^ bit) for i in range(size)])]
    ppermute x39 -> x40, starting transfers between devices: 48.3 us -> 42.2 us  [swap(): return lax.ppermute(x, axis, [(i, i ^ bit) for i in range(size)])]
  transfers between devices with their start and end apart: 39 -> 40, of which waited for: 29 -> 28; matrix products, arithmetic and copies ran while one was open for 0% -> 0% of each run, Pallas kernels for 19% -> 19%
where the time goes in v1:
time: 195 us
  waiting for transfers between devices  91.3 us (47%)
  Pallas kernels  59.3 us (30%)
  starting transfers between devices  42.2 us (22%)
    ppermute x40, waiting for transfers between devices, swap(): return lax.ppermute(x, axis, [(i, i ^ bit) for i in range(size)])  91.3 us
    ppermute x40, starting transfers between devices, swap(): return lax.ppermute(x, axis, [(i, i ^ bit) for i in range(size)])  42.2 us
    pallas_call x2, Pallas kernels, second_solve(): call(second_kernel, 'second_solve', 6000000000, 20 * HALF * cols, out_sha...  12.5 us
    pallas_call x4, Pallas kernels, product(): call(functools.partial(product_kernel, not before, scaled), 'product', 4...  11.2 us
    pallas_call x2, Pallas kernels, first_solve(): call(first_kernel, 'first_solve', 5000000000, 20 * HALF * cols, out_shape...  10.4 us
    pallas_call x3, Pallas kernels, left_product(): call(functools.partial(left_kernel, dims), 'left', 0, 4 * rows * cols, ou...  8.86 us
    pallas_call x1, Pallas kernels, update(): call(update_kernel, 'update', 8 * rows * cols * RANK, 8 * rows * cols, ou...  8.77 us
    pallas_call x1, Pallas kernels, start(): call(start_kernel, 'start', 4 * rows * cols * RANK, 6 * rows * cols, out_...  7.03 us
  transfers between devices with their start and end apart: 40, of which 28 were waited for; matrix products, arithmetic and copies ran while one was open for 0% of the time, Pallas kernels for 19%

profile of v1, /device:TPU:0, one launch (start us, length us, event | category | flops | bytes accessed | tf_op | source)
XLA Modules:
  0.0 194.9 jit_solution(14886322019804327928)
XLA Ops:
  0.6 7.0 %start.1 = (bf16[1024,2048]{1,0:T(8,128)(2,1)S(1)}, bf16[1024,2048]{1,0:T(8,128)(2,1)S(1)}, f32[512,128]{1,0:T(8,128)S(1)}, f32[512,128]{1,0:T(8,128)S(1)}, bf16[2048,256]{1,0:T(8,128)(2,1)S(1)}) custom-call(s32[1]{0:T(128)} %bitcast.me_ref, f32[1024,2048]{1,0:T(8,128)} %bitcast.6, bf16[1024,2048]{1,0:T(8,128)(2,1)} %bitcast.7, f32[2048,256]{1,0:T(8,128)} %basis_ref.1), custom_call_target="tpu_custom_call" | custom-call | flops 2147483648 | bytes 12582912 | tf_op jit(solution)/shard_map/start/pallas_call | solution.py:164
  7.7 3.0 %collective-permute-start = (f32[512,128]{1,0:T(8,128)S(1)}, f32[512,128]{1,0:T(8,128)S(1)}, u32[]{:S(2)}, u32[]{:S(2)}) collective-permute-start(f32[512,128]{1,0:T(8,128)S(1)} %get-tuple-element.129), channel_id=1, source_target_pairs={{0,1},{1,0},{2,3},{3,2},{4,5},{5,4},{6,7},{7,6},{8,9},{9,8},{10,11... | collective-permute-start | bytes 786440 | tf_op jit(solution)/shard_map/ppermute | solution.py:354
  12.2 2.9 %left.3 = (f32[512,128]{1,0:T(8,128)S(1)}, f32[512,128]{1,0:T(8,128)S(1)}) custom-call(bf16[1024,2048]{1,0:T(8,128)(2,1)S(1)} %get-tuple-element.124.high_ref.refs_4_.refs_5_, bf16[1024,2048]{1,0:T(8,128)(2,1)S(1)} %get-tuple-element.125.low_ref.refs_5_.refs_6_, bf16[2048,256]{1,0:T(8,128)(2,1)S(1)} %get-tuple-element.126.factor_ref), custom_call_target="tpu_custom_call" | custom-call | bytes 8388608 | tf_op jit(solution)/shard_map/left/pallas_call | solution.py:197
  20.7 4.7 %collective-permute-done.3.refs_3_ = f32[512,128]{1,0:T(8,128)S(1)} collective-permute-done((f32[512,128]{1,0:T(8,128)S(1)}, f32[512,128]{1,0:T(8,128)S(1)}, u32[]{:S(2)}, u32[]{:S(2)}) %collective-permute-start.3) | collective-permute-done | bytes 262176 | tf_op jit(solution)/shard_map/ppermute | solution.py:354
  37.7 4.8 %collective-permute-done.9.refs_4_ = f32[512,128]{1,0:T(8,128)S(1)} collective-permute-done((f32[512,128]{1,0:T(8,128)S(1)}, f32[512,128]{1,0:T(8,128)S(1)}, u32[]{:S(2)}, u32[]{:S(2)}) %collective-permute-start.9) | collective-permute-done | bytes 262176 | tf_op jit(solution)/shard_map/ppermute | solution.py:354
  42.9 3.5 %product.5 = (f32[64,2304]{1,0:T(8,128)S(1)}, f32[64,2304]{1,0:T(8,128)S(1)}, f32[1024,128]{1,0:T(8,128)}) custom-call(s32[1]{0:T(128)} %bitcast.me_ref, f32[1024,128]{1,0:T(8,128)S(1)} %get-tuple-element.146.refs_0_, f32[512,128]{1,0:T(8,128)S(1)} %add.70.refs_1_, f32[512,128]{1,0:T(8,128)S(1)} %collective-permute-done.8.refs_2_, ...), custom_call_target="tpu_custom_call" | custom-call | flops 2415919104 | bytes 9437184 | tf_op jit(solution)/shard_map/product/pallas_call | solution.py:241
  46.4 2.6 %collective-permute-start.10 = (f32[32,2176]{1,0:T(8,128)S(1)}, f32[32,2176]{1,0:T(8,128)S(1)}, u32[]{:S(2)}, u32[]{:S(2)}) collective-permute-start(f32[32,2176]{1,0:T(8,128)S(1)} %slice_add_fusion.1), channel_id=1, source_target_pairs={{0,16},{4,20},{8,24},{12,28},{16,0},{20,4},{24,8},{28,12},{1,17},{... | collective-permute-start | bytes 835592 | tf_op jit(solution)/shard_map/ppermute | solution.py:354
  51.2 11.3 %collective-permute-done.10 = f32[32,2176]{1,0:T(8,128)S(1)} collective-permute-done((f32[32,2176]{1,0:T(8,128)S(1)}, f32[32,2176]{1,0:T(8,128)S(1)}, u32[]{:S(2)}, u32[]{:S(2)}) %collective-permute-start.10) | collective-permute-done | bytes 278560 | tf_op jit(solution)/shard_map/ppermute | solution.py:354
  67.8 8.8 %collective-permute-done.14 = f32[32,2176]{1,0:T(8,128)S(1)} collective-permute-done((f32[32,2176]{1,0:T(8,128)S(1)}, f32[32,2176]{1,0:T(8,128)S(1)}, u32[]{:S(2)}, u32[]{:S(2)}) %collective-permute-start.14) | collective-permute-done | bytes 278560 | tf_op jit(solution)/shard_map/ppermute | solution.py:354
  80.5 5.6 %first_solve.2 = (f32[128,128]{1,0:T(8,128)S(1)}, f32[128,2048]{1,0:T(8,128)S(1)}, f32[128,2048]{1,0:T(8,128)}, bf16[256,2048]{1,0:T(8,128)(2,1)S(1)}, f32[8,128]{1,0:T(8,128)S(1)}) custom-call(s32[1]{0:T(128)} %bitcast.me_ref, f32[64,2176]{1,0:T(8,128)S(1)} %constant_dynamic-update-slice_fusion.mine_ref, f32[64,2176]{1,0:T(8,128)S(1)} %collective-permute-done.17.other_ref), custom_call_target="tpu_custom_call" | custom-call | flops 5000000000 | bytes 5242880 | tf_op jit(solution)/shard_map/first_solve/pallas_call | solution.py:272
  86.2 3.0 %left.4 = (f32[520,128]{1,0:T(8,128)S(1)}, f32[512,128]{1,0:T(8,128)S(1)}) custom-call(bf16[1024,2048]{1,0:T(8,128)(2,1)S(1)} %get-tuple-element.124.high_ref.refs_4_.refs_5_, bf16[1024,2048]{1,0:T(8,128)(2,1)S(1)} %get-tuple-element.125.low_ref.refs_5_.refs_6_, bf16[256,2048]{1,0:T(8,128)(2,1)S(1)} %get-tuple-element.168.factor_ref, ...), custom_call_target="tpu_custom_call" | custom-call | bytes 8388608 | tf_op jit(solution)/shard_map/left/pallas_call | solution.py:197
  92.7 6.6 %second_solve.2 = (f32[256,256]{1,0:T(8,128)}, f32[128,2048]{1,0:T(8,128)}, bf16[256,2048]{1,0:T(8,128)(2,1)S(1)}, f32[8,128]{1,0:T(8,128)S(1)}) custom-call(s32[1]{0:T(128)} %bitcast.me_ref, f32[64,2304]{1,0:T(8,128)S(1)} %constant_dynamic-update-slice_fusion.2.mine_ref, f32[64,2304]{1,0:T(8,128)S(1)} %collective-permute-done.20.other_ref, ...), custom_call_target="tpu_custom_call" | custom-call | flops 6000000000 | bytes 5242880 | tf_op jit(solution)/shard_map/second_solve/pallas_call | solution.py:296
  101.6 3.0 %left.5 = (f32[520,128]{1,0:T(8,128)S(1)}, f32[512,128]{1,0:T(8,128)S(1)}) custom-call(bf16[1024,2048]{1,0:T(8,128)(2,1)S(1)} %get-tuple-element.124.high_ref.refs_4_.refs_5_, bf16[1024,2048]{1,0:T(8,128)(2,1)S(1)} %get-tuple-element.125.low_ref.refs_5_.refs_6_, bf16[256,2048]{1,0:T(8,128)(2,1)S(1)} %get-tuple-element.184.factor_ref, ...), custom_call_target="tpu_custom_call" | custom-call | bytes 8388608 | tf_op jit(solution)/shard_map/left/pallas_call | solution.py:197
  104.6 3.4 %collective-permute-done.22.refs_3_ = f32[512,128]{1,0:T(8,128)S(1)} collective-permute-done((f32[512,128]{1,0:T(8,128)S(1)}, f32[512,128]{1,0:T(8,128)S(1)}, u32[]{:S(2)}, u32[]{:S(2)}) %collective-permute-start.22) | collective-permute-done | bytes 262176 | tf_op jit(solution)/shard_map/ppermute | solution.py:354
  113.0 3.2 %collective-permute-done.24 = f32[512,128]{1,0:T(8,128)S(1)} collective-permute-done((f32[512,128]{1,0:T(8,128)S(1)}, f32[512,128]{1,0:T(8,128)S(1)}, u32[]{:S(2)}, u32[]{:S(2)}) %collective-permute-start.24) | collective-permute-done | bytes 262176 | tf_op jit(solution)/shard_map/ppermute | solution.py:354
  118.3 7.2 %collective-permute-done.28.refs_4_ = f32[512,128]{1,0:T(8,128)S(1)} collective-permute-done((f32[512,128]{1,0:T(8,128)S(1)}, f32[512,128]{1,0:T(8,128)S(1)}, u32[]{:S(2)}, u32[]{:S(2)}) %collective-permute-start.28) | collective-permute-done | bytes 262176 | tf_op jit(solution)/shard_map/ppermute | solution.py:354
  125.5 2.9 %product.7 = (f32[64,2304]{1,0:T(8,128)S(1)}, f32[64,2304]{1,0:T(8,128)S(1)}, f32[1024,128]{1,0:T(8,128)S(1)}) custom-call(s32[1]{0:T(128)} %bitcast.me_ref, f32[1024,128]{1,0:T(8,128)S(1)} %get-tuple-element.199.refs_0_.left0_ref, f32[520,128]{1,0:T(8,128)S(1)} %add.80.refs_1_, f32[520,128]{1,0:T(8,128)S(1)} %collective-permute-done.27.refs_2_, ...), custom_call_target="tpu_custom_call" | custom-call | flops 2415919104 | bytes 9437184 | tf_op jit(solution)/shard_map/product/pallas_call | solution.py:241
  132.7 12.0 %collective-permute-done.29 = f32[32,2176]{1,0:T(8,128)S(1)} collective-permute-done((f32[32,2176]{1,0:T(8,128)S(1)}, f32[32,2176]{1,0:T(8,128)S(1)}, u32[]{:S(2)}, u32[]{:S(2)}) %collective-permute-start.29) | collective-permute-done | bytes 278560 | tf_op jit(solution)/shard_map/ppermute | solution.py:354
  149.0 9.1 %collective-permute-done.33 = f32[32,2176]{1,0:T(8,128)S(1)} collective-permute-done((f32[32,2176]{1,0:T(8,128)S(1)}, f32[32,2176]{1,0:T(8,128)S(1)}, u32[]{:S(2)}, u32[]{:S(2)}) %collective-permute-start.33) | collective-permute-done | bytes 278560 | tf_op jit(solution)/shard_map/ppermute | solution.py:354
  158.1 3.0 %collective-permute-done.34 = f32[32,2304]{1,0:T(8,128)S(1)} collective-permute-done((f32[32,2304]{1,0:T(8,128)S(1)}, f32[32,2304]{1,0:T(8,128)S(1)}, u32[]{:S(2)}, u32[]{:S(2)}) %collective-permute-start.34) | collective-permute-done | bytes 294944 | tf_op jit(solution)/shard_map/ppermute | solution.py:354
  163.2 4.8 %first_solve.3 = (f32[128,128]{1,0:T(8,128)S(1)}, f32[128,2048]{1,0:T(8,128)S(1)}, f32[128,2048]{1,0:T(8,128)S(1)}, bf16[256,2048]{1,0:T(8,128)(2,1)S(1)}, f32[8,128]{1,0:T(8,128)S(1)}) custom-call(s32[1]{0:T(128)} %bitcast.me_ref, f32[64,2176]{1,0:T(8,128)S(1)} %constant_dynamic-update-slice_fusion.4.mine_ref, f32[64,2176]{1,0:T(8,128)S(1)} %collective-permute-done.36.other_ref), custom_call_target="tpu_custom_call" | custom-call | flops 5000000000 | bytes 5242880 | tf_op jit(solution)/shard_map/first_solve/pallas_call | solution.py:272
  167.9 2.8 %collective-permute-done.35 = f32[32,2304]{1,0:T(8,128)S(1)} collective-permute-done((f32[32,2304]{1,0:T(8,128)S(1)}, f32[32,2304]{1,0:T(8,128)S(1)}, u32[]{:S(2)}, u32[]{:S(2)}) %collective-permute-start.35) | collective-permute-done | bytes 294944 | tf_op jit(solution)/shard_map/ppermute | solution.py:354
  172.9 5.9 %second_solve.3 = (f32[256,256]{1,0:T(8,128)S(1)}, f32[128,2048]{1,0:T(8,128)S(1)}, bf16[256,2048]{1,0:T(8,128)(2,1)S(1)}, f32[8,128]{1,0:T(8,128)S(1)}) custom-call(s32[1]{0:T(128)} %bitcast.me_ref, f32[64,2304]{1,0:T(8,128)S(1)} %constant_dynamic-update-slice_fusion.6.mine_ref, f32[64,2304]{1,0:T(8,128)S(1)} %collective-permute-done.37.other_ref, ...), custom_call_target="tpu_custom_call" | custom-call | flops 6000000000 | bytes 5242880 | tf_op jit(solution)/shard_map/second_solve/pallas_call | solution.py:296
  186.1 8.8 %update.1 = (f32[1024,2048]{1,0:T(8,128)}, f32[1024,2048]{1,0:T(8,128)}, f32[2048,256]{1,0:T(8,128)}) custom-call(f32[1024,256]{1,0:T(8,128)S(1)} %ortho.1.ortho_ref, f32[8,256]{1,0:T(8,128)S(1)} %add.87.s0, f32[8,256]{1,0:T(8,128)S(1)} %collective-permute-done.39.s1, bf16[256,2048]{1,0:T(8,128)(2,1)S(1)} %get-tuple-element.234.pair0_ref, ...), custom_call_target="tpu_custom_call" | custom-call | flops 4294967296 | bytes 16777216 | tf_op jit(solution)/shard_map/update/pallas_call | solution.py:344
  (110 shorter events, 64.2 us)
Async XLA Ops:
  7.7 9.3 %collective-permute-start = (f32[512,128]{1,0:T(8,128)S(1)}, f32[512,128]{1,0:T(8,128)S(1)}, u32[]{:S(2)}, u32[]{:S(2)}) collective-permute-start(f32[512,128]{1,0:T(8,128)S(1)} %get-tuple-element.129), channel_id=1, source_target_pairs={{0,1},{1,0},{2,3},{3,2},{4,5},{5,4},{6,7},{7,6},{8,9},{9,8},{10,11... | collective-permute-start | bytes 786440 | tf_op jit(solution)/shard_map/ppermute | solution.py:354
  33.7 8.8 %collective-permute-start.9 = (f32[512,128]{1,0:T(8,128)S(1)}, f32[512,128]{1,0:T(8,128)S(1)}, u32[]{:S(2)}, u32[]{:S(2)}) collective-permute-start(f32[512,128]{1,0:T(8,128)S(1)} %add.71.refs_3_), channel_id=1, source_target_pairs={{0,1},{1,0},{2,3},{3,2},{4,5},{5,4},{6,7},{7,6},{8,9},{9,8},{10,11... | collective-permute-start | bytes 786440 | tf_op jit(solution)/shard_map/ppermute | solution.py:354
  34.4 8.5 %collective-permute-start.8 = (f32[512,128]{1,0:T(8,128)S(1)}, f32[512,128]{1,0:T(8,128)S(1)}, u32[]{:S(2)}, u32[]{:S(2)}) collective-permute-start(f32[512,128]{1,0:T(8,128)S(1)} %add.70.refs_1_), channel_id=1, source_target_pairs={{0,2},{1,3},{2,0},{3,1},{4,6},{5,7},{6,4},{7,5},{8,10},{9,11},{10,... | collective-permute-start | bytes 786440 | tf_op jit(solution)/shard_map/ppermute | solution.py:354
  36.0 10.4 %collective-permute-start.7 = (f32[32,2176]{1,0:T(8,128)S(1)}, f32[32,2176]{1,0:T(8,128)S(1)}, u32[]{:S(2)}, u32[]{:S(2)}) collective-permute-start(f32[32,2176]{1,0:T(8,128)S(1)} %slice.40), channel_id=1, source_target_pairs={{0,8},{4,12},{8,0},{12,4},{16,24},{20,28},{24,16},{28,20},{1,9},{5... | collective-permute-start | bytes 835592 | tf_op jit(solution)/shard_map/ppermute | solution.py:354
  46.4 16.1 %collective-permute-start.10 = (f32[32,2176]{1,0:T(8,128)S(1)}, f32[32,2176]{1,0:T(8,128)S(1)}, u32[]{:S(2)}, u32[]{:S(2)}) collective-permute-start(f32[32,2176]{1,0:T(8,128)S(1)} %slice_add_fusion.1), channel_id=1, source_target_pairs={{0,16},{4,20},{8,24},{12,28},{16,0},{20,4},{24,8},{28,12},{1,17},{... | collective-permute-start | bytes 835592 | tf_op jit(solution)/shard_map/ppermute | solution.py:354
  49.1 13.4 %collective-permute-start.13 = (f32[16,2304]{1,0:T(8,128)S(1)}, f32[16,2304]{1,0:T(8,128)S(1)}, u32[]{:S(2)}, u32[]{:S(2)}) collective-permute-start(f32[16,2304]{1,0:T(8,128)S(1)} %get-tuple-element.243), channel_id=1, source_target_pairs={{0,8},{4,12},{8,0},{12,4},{16,24},{20,28},{24,16},{28,20},{1,9},{5... | collective-permute-start | bytes 442376 | tf_op jit(solution)/shard_map/ppermute | solution.py:354
  50.7 12.5 %collective-permute-start.12 = (f32[16,2304]{1,0:T(8,128)S(1)}, f32[16,2304]{1,0:T(8,128)S(1)}, u32[]{:S(2)}, u32[]{:S(2)}) collective-permute-start(f32[16,2304]{1,0:T(8,128)S(1)} %get-tuple-element.244), channel_id=1, source_target_pairs={{0,8},{4,12},{8,0},{12,4},{16,24},{20,28},{24,16},{28,20},{1,9},{5... | collective-permute-start | bytes 442376 | tf_op jit(solution)/shard_map/ppermute | solution.py:354
  63.3 15.2 %collective-permute-start.15 = (f32[32,2304]{1,0:T(8,128)S(1)}, f32[32,2304]{1,0:T(8,128)S(1)}, u32[]{:S(2)}, u32[]{:S(2)}) collective-permute-start(f32[32,2304]{1,0:T(8,128)S(1)} %maximum_add_fusion), channel_id=1, source_target_pairs={{0,16},{4,20},{8,24},{12,28},{16,0},{20,4},{24,8},{28,12},{1,17},{... | collective-permute-start | bytes 884744 | tf_op jit(solution)/shard_map/ppermute | solution.py:354
  65.2 11.4 %collective-permute-start.14 = (f32[32,2176]{1,0:T(8,128)S(1)}, f32[32,2176]{1,0:T(8,128)S(1)}, u32[]{:S(2)}, u32[]{:S(2)}) collective-permute-start(f32[32,2176]{1,0:T(8,128)S(1)} %add.74), channel_id=1, source_target_pairs={{0,8},{4,12},{8,0},{12,4},{16,24},{20,28},{24,16},{28,20},{1,9},{5... | collective-permute-start | bytes 835592 | tf_op jit(solution)/shard_map/ppermute | solution.py:354
  78.6 10.5 %collective-permute-start.16 = (f32[32,2304]{1,0:T(8,128)S(1)}, f32[32,2304]{1,0:T(8,128)S(1)}, u32[]{:S(2)}, u32[]{:S(2)}) collective-permute-start(f32[32,2304]{1,0:T(8,128)S(1)} %add.76), channel_id=1, source_target_pairs={{0,8},{4,12},{8,0},{12,4},{16,24},{20,28},{24,16},{28,20},{1,9},{5... | collective-permute-start | bytes 884744 | tf_op jit(solution)/shard_map/ppermute | solution.py:354
  89.4 9.9 %collective-permute-start.19 = (f32[512,128]{1,0:T(8,128)S(1)}, f32[512,128]{1,0:T(8,128)S(1)}, u32[]{:S(2)}, u32[]{:S(2)}) collective-permute-start(f32[512,128]{1,0:T(8,128)S(1)} %get-tuple-element.182), channel_id=1, source_target_pairs={{0,2},{1,3},{2,0},{3,1},{4,6},{5,7},{6,4},{7,5},{8,10},{9,11},{10,... | collective-permute-start | bytes 786440 | tf_op jit(solution)/shard_map/ppermute | solution.py:354
  91.3 8.4 %collective-permute-start.18 = (f32[520,128]{1,0:T(8,128)S(1)}, f32[520,128]{1,0:T(8,128)S(1)}, u32[]{:S(2)}, u32[]{:S(2)}) collective-permute-start(f32[520,128]{1,0:T(8,128)S(1)} %get-tuple-element.180), channel_id=1, source_target_pairs={{0,1},{1,0},{2,3},{3,2},{4,5},{5,4},{6,7},{7,6},{8,9},{9,8},{10,11... | collective-permute-start | bytes 798728 | tf_op jit(solution)/shard_map/ppermute | solution.py:354
  99.7 8.3 %collective-permute-start.21 = (f32[520,128]{1,0:T(8,128)S(1)}, f32[520,128]{1,0:T(8,128)S(1)}, u32[]{:S(2)}, u32[]{:S(2)}) collective-permute-start(f32[520,128]{1,0:T(8,128)S(1)} %add.77.refs_0_), channel_id=1, source_target_pairs={{0,2},{1,3},{2,0},{3,1},{4,6},{5,7},{6,4},{7,5},{8,10},{9,11},{10,... | collective-permute-start | bytes 798728 | tf_op jit(solution)/shard_map/ppermute | solution.py:354
  100.1 7.9 %collective-permute-start.22 = (f32[512,128]{1,0:T(8,128)S(1)}, f32[512,128]{1,0:T(8,128)S(1)}, u32[]{:S(2)}, u32[]{:S(2)}) collective-permute-start(f32[512,128]{1,0:T(8,128)S(1)} %add.78.refs_2_), channel_id=1, source_target_pairs={{0,1},{1,0},{2,3},{3,2},{4,5},{5,4},{6,7},{7,6},{8,9},{9,8},{10,11... | collective-permute-start | bytes 786440 | tf_op jit(solution)/shard_map/ppermute | solution.py:354
  108.0 8.1 %collective-permute-start.23 = (f32[520,128]{1,0:T(8,128)S(1)}, f32[520,128]{1,0:T(8,128)S(1)}, u32[]{:S(2)}, u32[]{:S(2)}) collective-permute-start(f32[520,128]{1,0:T(8,128)S(1)} %get-tuple-element.200), channel_id=1, source_target_pairs={{0,1},{1,0},{2,3},{3,2},{4,5},{5,4},{6,7},{7,6},{8,9},{9,8},{10,11... | collective-permute-start | bytes 798728 | tf_op jit(solution)/shard_map/ppermute | solution.py:354
  116.2 9.4 %collective-permute-start.27 = (f32[520,128]{1,0:T(8,128)S(1)}, f32[520,128]{1,0:T(8,128)S(1)}, u32[]{:S(2)}, u32[]{:S(2)}) collective-permute-start(f32[520,128]{1,0:T(8,128)S(1)} %add.80.refs_1_), channel_id=1, source_target_pairs={{0,2},{1,3},{2,0},{3,1},{4,6},{5,7},{6,4},{7,5},{8,10},{9,11},{10,... | collective-permute-start | bytes 798728 | tf_op jit(solution)/shard_map/ppermute | solution.py:354
  117.0 8.5 %collective-permute-start.28 = (f32[512,128]{1,0:T(8,128)S(1)}, f32[512,128]{1,0:T(8,128)S(1)}, u32[]{:S(2)}, u32[]{:S(2)}) collective-permute-start(f32[512,128]{1,0:T(8,128)S(1)} %add.81.refs_3_), channel_id=1, source_target_pairs={{0,1},{1,0},{2,3},{3,2},{4,5},{5,4},{6,7},{7,6},{8,9},{9,8},{10,11... | collective-permute-start | bytes 786440 | tf_op jit(solution)/shard_map/ppermute | solution.py:354
  118.2 10.2 %collective-permute-start.26 = (f32[32,2176]{1,0:T(8,128)S(1)}, f32[32,2176]{1,0:T(8,128)S(1)}, u32[]{:S(2)}, u32[]{:S(2)}) collective-permute-start(f32[32,2176]{1,0:T(8,128)S(1)} %slice.43), channel_id=1, source_target_pairs={{0,8},{4,12},{8,0},{12,4},{16,24},{20,28},{24,16},{28,20},{1,9},{5... | collective-permute-start | bytes 835592 | tf_op jit(solution)/shard_map/ppermute | solution.py:354
  128.5 16.1 %collective-permute-start.29 = (f32[32,2176]{1,0:T(8,128)S(1)}, f32[32,2176]{1,0:T(8,128)S(1)}, u32[]{:S(2)}, u32[]{:S(2)}) collective-permute-start(f32[32,2176]{1,0:T(8,128)S(1)} %slice_add_fusion), channel_id=1, source_target_pairs={{0,16},{4,20},{8,24},{12,28},{16,0},{20,4},{24,8},{28,12},{1,17},{... | collective-permute-start | bytes 835592 | tf_op jit(solution)/shard_map/ppermute | solution.py:354
  130.6 14.1 %collective-permute-start.32 = (f32[16,2304]{1,0:T(8,128)S(1)}, f32[16,2304]{1,0:T(8,128)S(1)}, u32[]{:S(2)}, u32[]{:S(2)}) collective-permute-start(f32[16,2304]{1,0:T(8,128)S(1)} %get-tuple-element.241), channel_id=1, source_target_pairs={{0,8},{4,12},{8,0},{12,4},{16,24},{20,28},{24,16},{28,20},{1,9},{5... | collective-permute-start | bytes 442376 | tf_op jit(solution)/shard_map/ppermute | solution.py:354
  132.0 13.6 %collective-permute-start.31 = (f32[16,2304]{1,0:T(8,128)S(1)}, f32[16,2304]{1,0:T(8,128)S(1)}, u32[]{:S(2)}, u32[]{:S(2)}) collective-permute-start(f32[16,2304]{1,0:T(8,128)S(1)} %get-tuple-element.242), channel_id=1, source_target_pairs={{0,8},{4,12},{8,0},{12,4},{16,24},{20,28},{24,16},{28,20},{1,9},{5... | collective-permute-start | bytes 442376 | tf_op jit(solution)/shard_map/ppermute | solution.py:354
  145.6 15.5 %collective-permute-start.34 = (f32[32,2304]{1,0:T(8,128)S(1)}, f32[32,2304]{1,0:T(8,128)S(1)}, u32[]{:S(2)}, u32[]{:S(2)}) collective-permute-start(f32[32,2304]{1,0:T(8,128)S(1)} %maximum_add_fusion.1), channel_id=1, source_target_pairs={{0,16},{4,20},{8,24},{12,28},{16,0},{20,4},{24,8},{28,12},{1,17},{... | collective-permute-start | bytes 884744 | tf_op jit(solution)/shard_map/ppermute | solution.py:354
  146.5 11.6 %collective-permute-start.33 = (f32[32,2176]{1,0:T(8,128)S(1)}, f32[32,2176]{1,0:T(8,128)S(1)}, u32[]{:S(2)}, u32[]{:S(2)}) collective-permute-start(f32[32,2176]{1,0:T(8,128)S(1)} %add.84), channel_id=1, source_target_pairs={{0,8},{4,12},{8,0},{12,4},{16,24},{20,28},{24,16},{28,20},{1,9},{5... | collective-permute-start | bytes 835592 | tf_op jit(solution)/shard_map/ppermute | solution.py:354
  161.3 9.5 %collective-permute-start.35 = (f32[32,2304]{1,0:T(8,128)S(1)}, f32[32,2304]{1,0:T(8,128)S(1)}, u32[]{:S(2)}, u32[]{:S(2)}) collective-permute-start(f32[32,2304]{1,0:T(8,128)S(1)} %add.86), channel_id=1, source_target_pairs={{0,8},{4,12},{8,0},{12,4},{16,24},{20,28},{24,16},{28,20},{1,9},{5... | collective-permute-start | bytes 884744 | tf_op jit(solution)/shard_map/ppermute | solution.py:354
  (18 other events, 97.4 us)

commit v2 on v0

--- a/solution.py
+++ b/solution.py
@@ -123,9 +123,8 @@
     )(gram)
 
 
-def place(out_ref, me, mine, other):
-    for b in range(4):
-        block = (mine, other)[b // 2][PART * (b % 2):PART * (b % 2 + 1), :]
+def place(out_ref, me, blocks):
+    for b, block in enumerate(blocks):
         out_ref[pl.ds(pl.multiple_of((me ^ b) * PART, PART), PART), :] = block
 
 
@@ -153,7 +152,7 @@
             up_ref[...] += part[:half]
             down_ref[...] += part[half:]
 
-    block = pl.BlockSpec((rows, STEP), lambda i: (0, i))
+    block = pl.BlockSpec((rows, STEP), lambda i: (0, i), pipeline_mode=pl.Buffered(3))
     pltpu.emit_pipeline(
         body, grid=(cols // STEP,), in_specs=[block, block, pl.BlockSpec((STEP, RANK), lambda i: (i, 0))],
     )(momentum_ref, gradient_ref, basis_ref)
@@ -259,27 +258,29 @@
     return jnp.broadcast_to(square, (HALF, HALF)).T[:SUB, :]
 
 
-def first_kernel(me_ref, mine_ref, other_ref, inverse_ref, wide_ref, out_ref, pair_ref, square_ref, gram_ref):
+def first_kernel(me_ref, *refs):
+    blocks, (inverse_ref, wide_ref, out_ref, pair_ref, square_ref, gram_ref) = refs[:4], refs[4:]
     me = me_ref[0]
-    place(gram_ref, me, mine_ref[:, :HALF], other_ref[:, :HALF])
-    place(wide_ref, me, mine_ref[:, HALF:], other_ref[:, HALF:])
+    place(gram_ref, me, [ref[:, :HALF] for ref in blocks])
+    place(wide_ref, me, [ref[:, HALF:] for ref in blocks])
     inverse_ref[...] = inverse_factor(gram_ref[...])
     square_ref[...] = solved(inverse_ref[...], wide_ref, out_ref, pair_ref)
 
 
-def first_solve(me, mine, other):
-    cols = mine.shape[1] - HALF
+def first_solve(me, blocks):
+    cols = blocks[0].shape[1] - HALF
     return call(
         first_kernel, "first_solve", 5_000_000_000, 20 * HALF * cols,
         out_shape=[shaped(HALF, HALF), shaped(HALF, cols), shaped(HALF, cols), shaped(RANK, cols, dtype=BF16), shaped(SUB, HALF)],
-        in_specs=[SMEM, VMEM, VMEM], out_specs=[VMEM] * 5, scratch_shapes=[pltpu.VMEM((HALF, HALF), F32)],
-    )(me, mine, other)
-
-
-def second_kernel(me_ref, mine_ref, other_ref, first_ref, wide0_ref, inverse_ref, out_ref, pair_ref, square_ref, gram_ref, wide_ref):
+        in_specs=[SMEM] + [VMEM] * 4, out_specs=[VMEM] * 5, scratch_shapes=[pltpu.VMEM((HALF, HALF), F32)],
+    )(me, *blocks)
+
+
+def second_kernel(me_ref, *refs):
+    blocks, (first_ref, wide0_ref, inverse_ref, out_ref, pair_ref, square_ref, gram_ref, wide_ref) = refs[:4], refs[4:]
     me = me_ref[0]
-    place(gram_ref, me, mine_ref[:, :RANK], other_ref[:, :RANK])
-    place(wide_ref.at[HALF:, :], me, mine_ref[:, RANK:], other_ref[:, RANK:])
+    place(gram_ref, me, [ref[:, :RANK] for ref in blocks])
+    place(wide_ref.at[HALF:, :], me, [ref[:, RANK:] for ref in blocks])
     wide_ref[:HALF, :] = wide0_ref[...]
     first = first_ref[...]
     side = dot(gram_ref[:, :HALF], first, NT, HIGHEST)
@@ -291,14 +292,14 @@
     square_ref[...] = solved(inverse_ref[HALF:, :], wide_ref, out_ref, pair_ref)
 
 
-def second_solve(me, mine, other, first, wide0):
-    cols = mine.shape[1] - RANK
+def second_solve(me, blocks, first, wide0):
+    cols = blocks[0].shape[1] - RANK
     return call(
         second_kernel, "second_solve", 6_000_000_000, 20 * HALF * cols,
         out_shape=[shaped(RANK, RANK), shaped(HALF, cols), shaped(RANK, cols, dtype=BF16), shaped(SUB, HALF)],
-        in_specs=[SMEM] + [VMEM] * 4, out_specs=[VMEM] * 4,
+        in_specs=[SMEM] + [VMEM] * 6, out_specs=[VMEM] * 4,
         scratch_shapes=[pltpu.VMEM((HALF, RANK), F32), pltpu.VMEM((RANK, cols), F32)],
-    )(me, mine, other, first, wide0)
+    )(me, *blocks, first, wide0)
 
 
 def ortho_kernel(left0_ref, left1_ref, inverse_ref, out_ref):
@@ -386,35 +387,31 @@
         keep1, give1, left1 = product(scaled, me, (left0,), (up1, got1[0], down1, got1[1]), buffer)
         part0, pair0, keep1, give1 = together(part0, pair0, keep1, give1)
 
-        core1 = swap(give1, "row", 1)
-        part0, pair0, keep1, core1 = together(part0, pair0, keep1, core1)
-
         side0 = part0[:PART] + pair0
         cross0 = swap(side0, "row", 4)
-        part1 = keep1 + core1
-        pair1 = swap(part1[PART:], "row", 2)
+        part1 = keep1 + swap(give1, "row", 1)
+        pair1 = [swap(part1[rows], "row", 2) for rows in (slice(PART, PART + PART // 2), slice(PART + PART // 2, None))]
         side0, cross0, part1, pair1 = together(side0, cross0, part1, pair1)
 
         total0 = side0 + cross0
         back0 = swap(total0, "row", 2)
-        side1 = part1[:PART] + pair1
+        others0 = swap(total0, "row", 1), swap(back0, "row", 1)
+        side1 = part1[:PART] + jnp.concatenate(pair1, axis=0)
         cross1 = swap(side1, "row", 4)
-        total0, back0, side1, cross1 = together(total0, back0, side1, cross1)
-
-        mine0 = jnp.concatenate([total0, back0], axis=0)
-        other0 = swap(mine0, "row", 1)
+        total0, back0, others0, side1, cross1 = together(total0, back0, others0, side1, cross1)
+
         total1 = side1 + cross1
-        back1 = swap(total1, "row", 2)
-        first, wide, factor0, split0, square0 = first_solve(me, mine0, other0)
+        back1, other1 = swap(total1, "row", 2), swap(total1, "row", 1)
+        first, wide, factor0, split0, square0 = first_solve(me, (total0, back0, *others0))
         if not last:
             up0, down0 = left_product(buffer, split0, square0)
-        total1, back1, first, wide, split0, square0, up0, down0 = together(total1, back1, first, wide, split0, square0, up0, down0)
-
-        mine1 = jnp.concatenate([total1, back1], axis=0)
-        other1 = swap(mine1, "row", 1)
+        total1, back1, other1, first, wide, split0, square0, up0, down0 = together(
+            total1, back1, other1, first, wide, split0, square0, up0, down0
+        )
+
         if not last:
             got0 = swap(up0, "col", 1), swap(down0, "col", 2)
-        inverse, factor1, split1, square1 = second_solve(me, mine1, other1, first, wide)
+        inverse, factor1, split1, square1 = second_solve(me, (total1, back1, other1, swap(back1, "row", 1)), first, wide)
         if not last:
             up0, down0, got0, split1, square1 = together(up0, down0, got0, split1, square1)
 

time: 194 us -> 194 us (level)
  waiting for transfers between devices: 84.2 us -> 87.9 us
  starting transfers between devices: 48.3 us -> 45.2 us
    ppermute x39 -> x45, waiting for transfers between devices: 84.2 us -> 87.9 us  [swap(): return lax.ppermute(x, axis, [(i, i ^ bit) for i in range(size)])]
    ppermute x39 -> x45, starting transfers between devices: 48.3 us -> 45.2 us  [swap(): return lax.ppermute(x, axis, [(i, i ^ bit) for i in range(size)])]
  transfers between devices with their start and end apart: 39 -> 45, of which waited for: 29 -> 25; matrix products, arithmetic and copies ran while one was open for 0% -> 0% of each run, Pallas kernels for 19% -> 19%
where the time goes in v2:
time: 194 us
  waiting for transfers between devices  87.9 us (45%)
  Pallas kernels  59.4 us (31%)
  starting transfers between devices  45.2 us (23%)
    ppermute x45, waiting for transfers between devices, swap(): return lax.ppermute(x, axis, [(i, i ^ bit) for i in range(size)])  87.9 us
    ppermute x45, starting transfers between devices, swap(): return lax.ppermute(x, axis, [(i, i ^ bit) for i in range(size)])  45.2 us
    pallas_call x2, Pallas kernels, second_solve(): call(second_kernel, 'second_solve', 6000000000, 20 * HALF * cols, out_sha...  12.5 us
    pallas_call x4, Pallas kernels, product(): call(functools.partial(product_kernel, not before, scaled), 'product', 4...  11.2 us
    pallas_call x2, Pallas kernels, first_solve(): call(first_kernel, 'first_solve', 5000000000, 20 * HALF * cols, out_shape...  10.4 us
    pallas_call x3, Pallas kernels, left_product(): call(functools.partial(left_kernel, dims), 'left', 0, 4 * rows * cols, ou...  8.86 us
    pallas_call x1, Pallas kernels, update(): call(update_kernel, 'update', 8 * rows * cols * RANK, 8 * rows * cols, ou...  8.77 us
    pallas_call x1, Pallas kernels, start(): call(start_kernel, 'start', 4 * rows * cols * RANK, 6 * rows * cols, out_...  7.05 us
  transfers between devices with their start and end apart: 45, of which 25 were waited for; matrix products, arithmetic and copies ran while one was open for 0% of the time, Pallas kernels for 19%

profile of v2, /device:TPU:0, one launch (start us, length us, event | category | flops | bytes accessed | tf_op | source)
XLA Modules:
  0.0 194.2 jit_solution(6822662421031024087)
XLA Ops:
  0.6 7.1 %start.1 = (bf16[1024,2048]{1,0:T(8,128)(2,1)S(1)}, bf16[1024,2048]{1,0:T(8,128)(2,1)S(1)}, f32[512,128]{1,0:T(8,128)S(1)}, f32[512,128]{1,0:T(8,128)S(1)}, bf16[2048,256]{1,0:T(8,128)(2,1)S(1)}) custom-call(s32[1]{0:T(128)} %bitcast.me_ref, f32[1024,2048]{1,0:T(8,128)} %bitcast.6, bf16[1024,2048]{1,0:T(8,128)(2,1)} %bitcast.7, f32[2048,256]{1,0:T(8,128)} %basis_ref.1), custom_call_target="tpu_custom_call" | custom-call | flops 2147483648 | bytes 12582912 | tf_op jit(solution)/shard_map/start/pallas_call | solution.py:163
  7.7 3.0 %collective-permute-start = (f32[512,128]{1,0:T(8,128)S(1)}, f32[512,128]{1,0:T(8,128)S(1)}, u32[]{:S(2)}, u32[]{:S(2)}) collective-permute-start(f32[512,128]{1,0:T(8,128)S(1)} %get-tuple-element.136), channel_id=1, source_target_pairs={{0,1},{1,0},{2,3},{3,2},{4,5},{5,4},{6,7},{7,6},{8,9},{9,8},{10,11... | collective-permute-start | bytes 786440 | tf_op jit(solution)/shard_map/ppermute | solution.py:355
  12.2 2.9 %left.3 = (f32[512,128]{1,0:T(8,128)S(1)}, f32[512,128]{1,0:T(8,128)S(1)}) custom-call(bf16[1024,2048]{1,0:T(8,128)(2,1)S(1)} %get-tuple-element.131.high_ref.refs_4_.refs_5_, bf16[1024,2048]{1,0:T(8,128)(2,1)S(1)} %get-tuple-element.132.low_ref.refs_5_.refs_6_, bf16[2048,256]{1,0:T(8,128)(2,1)S(1)} %get-tuple-element.133.factor_ref), custom_call_target="tpu_custom_call" | custom-call | bytes 8388608 | tf_op jit(solution)/shard_map/left/pallas_call | solution.py:196
  20.7 4.7 %collective-permute-done.3.refs_3_ = f32[512,128]{1,0:T(8,128)S(1)} collective-permute-done((f32[512,128]{1,0:T(8,128)S(1)}, f32[512,128]{1,0:T(8,128)S(1)}, u32[]{:S(2)}, u32[]{:S(2)}) %collective-permute-start.3) | collective-permute-done | bytes 262176 | tf_op jit(solution)/shard_map/ppermute | solution.py:355
  37.7 4.8 %collective-permute-done.9.refs_4_ = f32[512,128]{1,0:T(8,128)S(1)} collective-permute-done((f32[512,128]{1,0:T(8,128)S(1)}, f32[512,128]{1,0:T(8,128)S(1)}, u32[]{:S(2)}, u32[]{:S(2)}) %collective-permute-start.9) | collective-permute-done | bytes 262176 | tf_op jit(solution)/shard_map/ppermute | solution.py:355
  43.0 3.5 %product.5 = (f32[64,2304]{1,0:T(8,128)S(1)}, f32[64,2304]{1,0:T(8,128)S(1)}, f32[1024,128]{1,0:T(8,128)}) custom-call(s32[1]{0:T(128)} %bitcast.me_ref, f32[1024,128]{1,0:T(8,128)S(1)} %get-tuple-element.153.refs_0_, f32[512,128]{1,0:T(8,128)S(1)} %add.67.refs_1_, f32[512,128]{1,0:T(8,128)S(1)} %collective-permute-done.8.refs_2_, ...), custom_call_target="tpu_custom_call" | custom-call | flops 2415919104 | bytes 9437184 | tf_op jit(solution)/shard_map/product/pallas_call | solution.py:240
  51.2 11.3 %collective-permute-done.10 = f32[32,2176]{1,0:T(8,128)S(1)} collective-permute-done((f32[32,2176]{1,0:T(8,128)S(1)}, f32[32,2176]{1,0:T(8,128)S(1)}, u32[]{:S(2)}, u32[]{:S(2)}) %collective-permute-start.10) | collective-permute-done | bytes 278560 | tf_op jit(solution)/shard_map/ppermute | solution.py:355
  64.6 3.2 %collective-permute-start.17 = (f32[32,2304]{1,0:T(8,128)S(1)}, f32[32,2304]{1,0:T(8,128)S(1)}, u32[]{:S(2)}, u32[]{:S(2)}) collective-permute-start(f32[32,2304]{1,0:T(8,128)S(1)} %maximum_add_fusion), channel_id=1, source_target_pairs={{0,16},{4,20},{8,24},{12,28},{16,0},{20,4},{24,8},{28,12},{1,17},{... | collective-permute-start | bytes 884744 | tf_op jit(solution)/shard_map/ppermute | solution.py:355
  67.8 9.2 %collective-permute-done.14.refs_1_ = f32[32,2176]{1,0:T(8,128)S(1)} collective-permute-done((f32[32,2176]{1,0:T(8,128)S(1)}, f32[32,2176]{1,0:T(8,128)S(1)}, u32[]{:S(2)}, u32[]{:S(2)}) %collective-permute-start.14) | collective-permute-done | bytes 278560 | tf_op jit(solution)/shard_map/ppermute | solution.py:355
  77.0 3.4 %collective-permute-done.17 = f32[32,2304]{1,0:T(8,128)S(1)} collective-permute-done((f32[32,2304]{1,0:T(8,128)S(1)}, f32[32,2304]{1,0:T(8,128)S(1)}, u32[]{:S(2)}, u32[]{:S(2)}) %collective-permute-start.17) | collective-permute-done | bytes 294944 | tf_op jit(solution)/shard_map/ppermute | solution.py:355
  80.6 5.7 %first_solve.2 = (f32[128,128]{1,0:T(8,128)S(1)}, f32[128,2048]{1,0:T(8,128)S(1)}, f32[128,2048]{1,0:T(8,128)}, bf16[256,2048]{1,0:T(8,128)(2,1)S(1)}, f32[8,128]{1,0:T(8,128)S(1)}) custom-call(s32[1]{0:T(128)} %bitcast.me_ref, f32[32,2176]{1,0:T(8,128)S(1)} %add.71.refs_0_, f32[32,2176]{1,0:T(8,128)S(1)} %collective-permute-done.14.refs_1_, ...), custom_call_target="tpu_custom_call" | custom-call | flops 5000000000 | bytes 5242880 | tf_op jit(solution)/shard_map/first_solve/pallas_call | solution.py:272
  86.2 3.0 %left.4 = (f32[520,128]{1,0:T(8,128)S(1)}, f32[512,128]{1,0:T(8,128)S(1)}) custom-call(bf16[1024,2048]{1,0:T(8,128)(2,1)S(1)} %get-tuple-element.131.high_ref.refs_4_.refs_5_, bf16[1024,2048]{1,0:T(8,128)(2,1)S(1)} %get-tuple-element.132.low_ref.refs_5_.refs_6_, bf16[256,2048]{1,0:T(8,128)(2,1)S(1)} %get-tuple-element.177.factor_ref, ...), custom_call_target="tpu_custom_call" | custom-call | bytes 8388608 | tf_op jit(solution)/shard_map/left/pallas_call | solution.py:196
  92.9 6.6 %second_solve.2 = (f32[256,256]{1,0:T(8,128)}, f32[128,2048]{1,0:T(8,128)}, bf16[256,2048]{1,0:T(8,128)(2,1)S(1)}, f32[8,128]{1,0:T(8,128)S(1)}) custom-call(s32[1]{0:T(128)} %bitcast.me_ref, f32[32,2304]{1,0:T(8,128)S(1)} %add.73.refs_0_, f32[32,2304]{1,0:T(8,128)S(1)} %collective-permute-done.18.refs_1_, f32[32,2304]{1,0:T(8,128)S(1)} %collective-permute-done.19.refs_2_, ...), custom_call_target="tpu_custom_call" | custom-call | flops 6000000000 | bytes 5242880 | tf_op jit(solution)/shard_map/second_solve/pallas_call | solution.py:297
  102.1 3.0 %left.5 = (f32[520,128]{1,0:T(8,128)S(1)}, f32[512,128]{1,0:T(8,128)S(1)}) custom-call(bf16[1024,2048]{1,0:T(8,128)(2,1)S(1)} %get-tuple-element.131.high_ref.refs_4_.refs_5_, bf16[1024,2048]{1,0:T(8,128)(2,1)S(1)} %get-tuple-element.132.low_ref.refs_5_.refs_6_, bf16[256,2048]{1,0:T(8,128)(2,1)S(1)} %get-tuple-element.194.factor_ref, ...), custom_call_target="tpu_custom_call" | custom-call | bytes 8388608 | tf_op jit(solution)/shard_map/left/pallas_call | solution.py:196
  105.1 3.0 %collective-permute-done.24.refs_3_ = f32[512,128]{1,0:T(8,128)S(1)} collective-permute-done((f32[512,128]{1,0:T(8,128)S(1)}, f32[512,128]{1,0:T(8,128)S(1)}, u32[]{:S(2)}, u32[]{:S(2)}) %collective-permute-start.24) | collective-permute-done | bytes 262176 | tf_op jit(solution)/shard_map/ppermute | solution.py:355
  119.8 6.3 %collective-permute-done.28.refs_4_ = f32[512,128]{1,0:T(8,128)S(1)} collective-permute-done((f32[512,128]{1,0:T(8,128)S(1)}, f32[512,128]{1,0:T(8,128)S(1)}, u32[]{:S(2)}, u32[]{:S(2)}) %collective-permute-start.28) | collective-permute-done | bytes 262176 | tf_op jit(solution)/shard_map/ppermute | solution.py:355
  126.0 2.9 %product.7 = (f32[64,2304]{1,0:T(8,128)S(1)}, f32[64,2304]{1,0:T(8,128)S(1)}, f32[1024,128]{1,0:T(8,128)S(1)}) custom-call(s32[1]{0:T(128)} %bitcast.me_ref, f32[1024,128]{1,0:T(8,128)S(1)} %get-tuple-element.207.refs_0_.left0_ref, f32[520,128]{1,0:T(8,128)S(1)} %add.76.refs_1_, f32[520,128]{1,0:T(8,128)S(1)} %collective-permute-done.27.refs_2_, ...), custom_call_target="tpu_custom_call" | custom-call | flops 2415919104 | bytes 9437184 | tf_op jit(solution)/shard_map/product/pallas_call | solution.py:240
  133.4 11.7 %collective-permute-done.31 = f32[32,2176]{1,0:T(8,128)S(1)} collective-permute-done((f32[32,2176]{1,0:T(8,128)S(1)}, f32[32,2176]{1,0:T(8,128)S(1)}, u32[]{:S(2)}, u32[]{:S(2)}) %collective-permute-start.31) | collective-permute-done | bytes 278560 | tf_op jit(solution)/shard_map/ppermute | solution.py:355
  148.6 9.6 %collective-permute-done.35.refs_1_ = f32[32,2176]{1,0:T(8,128)S(1)} collective-permute-done((f32[32,2176]{1,0:T(8,128)S(1)}, f32[32,2176]{1,0:T(8,128)S(1)}, u32[]{:S(2)}, u32[]{:S(2)}) %collective-permute-start.35) | collective-permute-done | bytes 278560 | tf_op jit(solution)/shard_map/ppermute | solution.py:355
  158.1 4.3 %collective-permute-done.38 = f32[32,2304]{1,0:T(8,128)S(1)} collective-permute-done((f32[32,2304]{1,0:T(8,128)S(1)}, f32[32,2304]{1,0:T(8,128)S(1)}, u32[]{:S(2)}, u32[]{:S(2)}) %collective-permute-start.38) | collective-permute-done | bytes 294944 | tf_op jit(solution)/shard_map/ppermute | solution.py:355
  162.6 4.8 %first_solve.3 = (f32[128,128]{1,0:T(8,128)S(1)}, f32[128,2048]{1,0:T(8,128)S(1)}, f32[128,2048]{1,0:T(8,128)S(1)}, bf16[256,2048]{1,0:T(8,128)(2,1)S(1)}, f32[8,128]{1,0:T(8,128)S(1)}) custom-call(s32[1]{0:T(128)} %bitcast.me_ref, f32[32,2176]{1,0:T(8,128)S(1)} %add.81.refs_0_, f32[32,2176]{1,0:T(8,128)S(1)} %collective-permute-done.35.refs_1_, ...), custom_call_target="tpu_custom_call" | custom-call | flops 5000000000 | bytes 5242880 | tf_op jit(solution)/shard_map/first_solve/pallas_call | solution.py:272
  167.4 4.6 %collective-permute-done.39.refs_1_ = f32[32,2304]{1,0:T(8,128)S(1)} collective-permute-done((f32[32,2304]{1,0:T(8,128)S(1)}, f32[32,2304]{1,0:T(8,128)S(1)}, u32[]{:S(2)}, u32[]{:S(2)}) %collective-permute-start.39) | collective-permute-done | bytes 294944 | tf_op jit(solution)/shard_map/ppermute | solution.py:355
  173.5 5.9 %second_solve.3 = (f32[256,256]{1,0:T(8,128)S(1)}, f32[128,2048]{1,0:T(8,128)S(1)}, bf16[256,2048]{1,0:T(8,128)(2,1)S(1)}, f32[8,128]{1,0:T(8,128)S(1)}) custom-call(s32[1]{0:T(128)} %bitcast.me_ref, f32[32,2304]{1,0:T(8,128)S(1)} %add.83.refs_0_, f32[32,2304]{1,0:T(8,128)S(1)} %collective-permute-done.39.refs_1_, ...), custom_call_target="tpu_custom_call" | custom-call | flops 6000000000 | bytes 5242880 | tf_op jit(solution)/shard_map/second_solve/pallas_call | solution.py:297
  185.4 8.8 %update.1 = (f32[1024,2048]{1,0:T(8,128)}, f32[1024,2048]{1,0:T(8,128)}, f32[2048,256]{1,0:T(8,128)}) custom-call(f32[1024,256]{1,0:T(8,128)S(1)} %ortho.1.ortho_ref, f32[8,256]{1,0:T(8,128)S(1)} %constant_dynamic-update-slice_fusion.s0, f32[8,256]{1,0:T(8,128)S(1)} %collective-permute-done.42.s1, f32[8,256]{1,0:T(8,128)S(1)} %collective-permute-done.43.s2, ...), custom_call_target="tpu_custom_call" | custom-call | flops 4294967296 | bytes 16777216 | tf_op jit(solution)/shard_map/update/pallas_call | solution.py:345
  (111 shorter events, 60.4 us)
Async XLA Ops:
  7.7 9.3 %collective-permute-start = (f32[512,128]{1,0:T(8,128)S(1)}, f32[512,128]{1,0:T(8,128)S(1)}, u32[]{:S(2)}, u32[]{:S(2)}) collective-permute-start(f32[512,128]{1,0:T(8,128)S(1)} %get-tuple-element.136), channel_id=1, source_target_pairs={{0,1},{1,0},{2,3},{3,2},{4,5},{5,4},{6,7},{7,6},{8,9},{9,8},{10,11... | collective-permute-start | bytes 786440 | tf_op jit(solution)/shard_map/ppermute | solution.py:355
  33.7 8.8 %collective-permute-start.9 = (f32[512,128]{1,0:T(8,128)S(1)}, f32[512,128]{1,0:T(8,128)S(1)}, u32[]{:S(2)}, u32[]{:S(2)}) collective-permute-start(f32[512,128]{1,0:T(8,128)S(1)} %add.68.refs_3_), channel_id=1, source_target_pairs={{0,1},{1,0},{2,3},{3,2},{4,5},{5,4},{6,7},{7,6},{8,9},{9,8},{10,11... | collective-permute-start | bytes 786440 | tf_op jit(solution)/shard_map/ppermute | solution.py:355
  34.4 8.5 %collective-permute-start.8 = (f32[512,128]{1,0:T(8,128)S(1)}, f32[512,128]{1,0:T(8,128)S(1)}, u32[]{:S(2)}, u32[]{:S(2)}) collective-permute-start(f32[512,128]{1,0:T(8,128)S(1)} %add.67.refs_1_), channel_id=1, source_target_pairs={{0,2},{1,3},{2,0},{3,1},{4,6},{5,7},{6,4},{7,5},{8,10},{9,11},{10,... | collective-permute-start | bytes 786440 | tf_op jit(solution)/shard_map/ppermute | solution.py:355
  36.0 10.4 %collective-permute-start.7 = (f32[32,2176]{1,0:T(8,128)S(1)}, f32[32,2176]{1,0:T(8,128)S(1)}, u32[]{:S(2)}, u32[]{:S(2)}) collective-permute-start(f32[32,2176]{1,0:T(8,128)S(1)} %slice.40), channel_id=1, source_target_pairs={{0,8},{4,12},{8,0},{12,4},{16,24},{20,28},{24,16},{28,20},{1,9},{5... | collective-permute-start | bytes 835592 | tf_op jit(solution)/shard_map/ppermute | solution.py:355
  46.4 16.1 %collective-permute-start.10 = (f32[32,2176]{1,0:T(8,128)S(1)}, f32[32,2176]{1,0:T(8,128)S(1)}, u32[]{:S(2)}, u32[]{:S(2)}) collective-permute-start(f32[32,2176]{1,0:T(8,128)S(1)} %slice_add_fusion.1), channel_id=1, source_target_pairs={{0,16},{4,20},{8,24},{12,28},{16,0},{20,4},{24,8},{28,12},{1,17},{... | collective-permute-start | bytes 835592 | tf_op jit(solution)/shard_map/ppermute | solution.py:355
  49.1 13.4 %collective-permute-start.13 = (f32[16,2304]{1,0:T(8,128)S(1)}, f32[16,2304]{1,0:T(8,128)S(1)}, u32[]{:S(2)}, u32[]{:S(2)}) collective-permute-start(f32[16,2304]{1,0:T(8,128)S(1)} %get-tuple-element.257), channel_id=1, source_target_pairs={{0,8},{4,12},{8,0},{12,4},{16,24},{20,28},{24,16},{28,20},{1,9},{5... | collective-permute-start | bytes 442376 | tf_op jit(solution)/shard_map/ppermute | solution.py:355
  50.8 12.5 %collective-permute-start.12 = (f32[16,2304]{1,0:T(8,128)S(1)}, f32[16,2304]{1,0:T(8,128)S(1)}, u32[]{:S(2)}, u32[]{:S(2)}) collective-permute-start(f32[16,2304]{1,0:T(8,128)S(1)} %get-tuple-element.258), channel_id=1, source_target_pairs={{0,8},{4,12},{8,0},{12,4},{16,24},{20,28},{24,16},{28,20},{1,9},{5... | collective-permute-start | bytes 442376 | tf_op jit(solution)/shard_map/ppermute | solution.py:355
  63.3 13.7 %collective-permute-start.14 = (f32[32,2176]{1,0:T(8,128)S(1)}, f32[32,2176]{1,0:T(8,128)S(1)}, u32[]{:S(2)}, u32[]{:S(2)}) collective-permute-start(f32[32,2176]{1,0:T(8,128)S(1)} %add.71.refs_0_), channel_id=1, source_target_pairs={{0,8},{4,12},{8,0},{12,4},{16,24},{20,28},{24,16},{28,20},{1,9},{5... | collective-permute-start | bytes 835592 | tf_op jit(solution)/shard_map/ppermute | solution.py:355
  64.6 15.8 %collective-permute-start.17 = (f32[32,2304]{1,0:T(8,128)S(1)}, f32[32,2304]{1,0:T(8,128)S(1)}, u32[]{:S(2)}, u32[]{:S(2)}) collective-permute-start(f32[32,2304]{1,0:T(8,128)S(1)} %maximum_add_fusion), channel_id=1, source_target_pairs={{0,16},{4,20},{8,24},{12,28},{16,0},{20,4},{24,8},{28,12},{1,17},{... | collective-permute-start | bytes 884744 | tf_op jit(solution)/shard_map/ppermute | solution.py:355
  67.8 9.2 %collective-permute-start.15 = (f32[32,2176]{1,0:T(8,128)S(1)}, f32[32,2176]{1,0:T(8,128)S(1)}, u32[]{:S(2)}, u32[]{:S(2)}) collective-permute-start(f32[32,2176]{1,0:T(8,128)S(1)} %add.71.refs_0_), channel_id=1, source_target_pairs={{0,4},{4,0},{8,12},{12,8},{16,20},{20,16},{24,28},{28,24},{1,5},{5... | collective-permute-start | bytes 835592 | tf_op jit(solution)/shard_map/ppermute | solution.py:355
  80.4 8.8 %collective-permute-start.19 = (f32[32,2304]{1,0:T(8,128)S(1)}, f32[32,2304]{1,0:T(8,128)S(1)}, u32[]{:S(2)}, u32[]{:S(2)}) collective-permute-start(f32[32,2304]{1,0:T(8,128)S(1)} %add.73.refs_0_), channel_id=1, source_target_pairs={{0,4},{4,0},{8,12},{12,8},{16,20},{20,16},{24,28},{28,24},{1,5},{5... | collective-permute-start | bytes 884744 | tf_op jit(solution)/shard_map/ppermute | solution.py:355
  80.5 9.4 %collective-permute-start.18 = (f32[32,2304]{1,0:T(8,128)S(1)}, f32[32,2304]{1,0:T(8,128)S(1)}, u32[]{:S(2)}, u32[]{:S(2)}) collective-permute-start(f32[32,2304]{1,0:T(8,128)S(1)} %add.73.refs_0_), channel_id=1, source_target_pairs={{0,8},{4,12},{8,0},{12,4},{16,24},{20,28},{24,16},{28,20},{1,9},{5... | collective-permute-start | bytes 884744 | tf_op jit(solution)/shard_map/ppermute | solution.py:355
  89.9 9.5 %collective-permute-start.21 = (f32[512,128]{1,0:T(8,128)S(1)}, f32[512,128]{1,0:T(8,128)S(1)}, u32[]{:S(2)}, u32[]{:S(2)}) collective-permute-start(f32[512,128]{1,0:T(8,128)S(1)} %get-tuple-element.192), channel_id=1, source_target_pairs={{0,2},{1,3},{2,0},{3,1},{4,6},{5,7},{6,4},{7,5},{8,10},{9,11},{10,... | collective-permute-start | bytes 786440 | tf_op jit(solution)/shard_map/ppermute | solution.py:355
  91.5 8.5 %collective-permute-start.20 = (f32[520,128]{1,0:T(8,128)S(1)}, f32[520,128]{1,0:T(8,128)S(1)}, u32[]{:S(2)}, u32[]{:S(2)}) collective-permute-start(f32[520,128]{1,0:T(8,128)S(1)} %get-tuple-element.190), channel_id=1, source_target_pairs={{0,1},{1,0},{2,3},{3,2},{4,5},{5,4},{6,7},{7,6},{8,9},{9,8},{10,11... | collective-permute-start | bytes 798728 | tf_op jit(solution)/shard_map/ppermute | solution.py:355
  115.9 10.1 %collective-permute-start.27 = (f32[520,128]{1,0:T(8,128)S(1)}, f32[520,128]{1,0:T(8,128)S(1)}, u32[]{:S(2)}, u32[]{:S(2)}) collective-permute-start(f32[520,128]{1,0:T(8,128)S(1)} %add.76.refs_1_), channel_id=1, source_target_pairs={{0,2},{1,3},{2,0},{3,1},{4,6},{5,7},{6,4},{7,5},{8,10},{9,11},{10,... | collective-permute-start | bytes 798728 | tf_op jit(solution)/shard_map/ppermute | solution.py:355
  117.5 8.5 %collective-permute-start.28 = (f32[512,128]{1,0:T(8,128)S(1)}, f32[512,128]{1,0:T(8,128)S(1)}, u32[]{:S(2)}, u32[]{:S(2)}) collective-permute-start(f32[512,128]{1,0:T(8,128)S(1)} %add.77.refs_3_), channel_id=1, source_target_pairs={{0,1},{1,0},{2,3},{3,2},{4,5},{5,4},{6,7},{7,6},{8,9},{9,8},{10,11... | collective-permute-start | bytes 786440 | tf_op jit(solution)/shard_map/ppermute | solution.py:355
  118.3 10.6 %collective-permute-start.30 = (f32[32,2176]{1,0:T(8,128)S(1)}, f32[32,2176]{1,0:T(8,128)S(1)}, u32[]{:S(2)}, u32[]{:S(2)}) collective-permute-start(f32[32,2176]{1,0:T(8,128)S(1)} %slice.43), channel_id=1, source_target_pairs={{0,8},{4,12},{8,0},{12,4},{16,24},{20,28},{24,16},{28,20},{1,9},{5... | collective-permute-start | bytes 835592 | tf_op jit(solution)/shard_map/ppermute | solution.py:355
  129.0 16.1 %collective-permute-start.31 = (f32[32,2176]{1,0:T(8,128)S(1)}, f32[32,2176]{1,0:T(8,128)S(1)}, u32[]{:S(2)}, u32[]{:S(2)}) collective-permute-start(f32[32,2176]{1,0:T(8,128)S(1)} %slice_add_fusion), channel_id=1, source_target_pairs={{0,16},{4,20},{8,24},{12,28},{16,0},{20,4},{24,8},{28,12},{1,17},{... | collective-permute-start | bytes 835592 | tf_op jit(solution)/shard_map/ppermute | solution.py:355
  131.3 13.8 %collective-permute-start.34 = (f32[16,2304]{1,0:T(8,128)S(1)}, f32[16,2304]{1,0:T(8,128)S(1)}, u32[]{:S(2)}, u32[]{:S(2)}) collective-permute-start(f32[16,2304]{1,0:T(8,128)S(1)} %get-tuple-element.255), channel_id=1, source_target_pairs={{0,8},{4,12},{8,0},{12,4},{16,24},{20,28},{24,16},{28,20},{1,9},{5... | collective-permute-start | bytes 442376 | tf_op jit(solution)/shard_map/ppermute | solution.py:355
  132.3 13.4 %collective-permute-start.33 = (f32[16,2304]{1,0:T(8,128)S(1)}, f32[16,2304]{1,0:T(8,128)S(1)}, u32[]{:S(2)}, u32[]{:S(2)}) collective-permute-start(f32[16,2304]{1,0:T(8,128)S(1)} %get-tuple-element.256), channel_id=1, source_target_pairs={{0,8},{4,12},{8,0},{12,4},{16,24},{20,28},{24,16},{28,20},{1,9},{5... | collective-permute-start | bytes 442376 | tf_op jit(solution)/shard_map/ppermute | solution.py:355
  145.7 12.4 %collective-permute-start.35 = (f32[32,2176]{1,0:T(8,128)S(1)}, f32[32,2176]{1,0:T(8,128)S(1)}, u32[]{:S(2)}, u32[]{:S(2)}) collective-permute-start(f32[32,2176]{1,0:T(8,128)S(1)} %add.81.refs_0_), channel_id=1, source_target_pairs={{0,8},{4,12},{8,0},{12,4},{16,24},{20,28},{24,16},{28,20},{1,9},{5... | collective-permute-start | bytes 835592 | tf_op jit(solution)/shard_map/ppermute | solution.py:355
  146.7 15.7 %collective-permute-start.38 = (f32[32,2304]{1,0:T(8,128)S(1)}, f32[32,2304]{1,0:T(8,128)S(1)}, u32[]{:S(2)}, u32[]{:S(2)}) collective-permute-start(f32[32,2304]{1,0:T(8,128)S(1)} %maximum_add_fusion.1), channel_id=1, source_target_pairs={{0,16},{4,20},{8,24},{12,28},{16,0},{20,4},{24,8},{28,12},{1,17},{... | collective-permute-start | bytes 884744 | tf_op jit(solution)/shard_map/ppermute | solution.py:355
  148.6 9.6 %collective-permute-start.36 = (f32[32,2176]{1,0:T(8,128)S(1)}, f32[32,2176]{1,0:T(8,128)S(1)}, u32[]{:S(2)}, u32[]{:S(2)}) collective-permute-start(f32[32,2176]{1,0:T(8,128)S(1)} %add.81.refs_0_), channel_id=1, source_target_pairs={{0,4},{4,0},{8,12},{12,8},{16,20},{20,16},{24,28},{28,24},{1,5},{5... | collective-permute-start | bytes 835592 | tf_op jit(solution)/shard_map/ppermute | solution.py:355
  162.5 9.4 %collective-permute-start.39 = (f32[32,2304]{1,0:T(8,128)S(1)}, f32[32,2304]{1,0:T(8,128)S(1)}, u32[]{:S(2)}, u32[]{:S(2)}) collective-permute-start(f32[32,2304]{1,0:T(8,128)S(1)} %add.83.refs_0_), channel_id=1, source_target_pairs={{0,8},{4,12},{8,0},{12,4},{16,24},{20,28},{24,16},{28,20},{1,9},{5... | collective-permute-start | bytes 884744 | tf_op jit(solution)/shard_map/ppermute | solution.py:355
  (23 other events, 129.8 us)

commit v3 on v2

--- a/solution.py
+++ b/solution.py
@@ -152,7 +152,7 @@
             up_ref[...] += part[:half]
             down_ref[...] += part[half:]
 
-    block = pl.BlockSpec((rows, STEP), lambda i: (0, i), pipeline_mode=pl.Buffered(3))
+    block = pl.BlockSpec((rows, STEP), lambda i: (0, i))
     pltpu.emit_pipeline(
         body, grid=(cols // STEP,), in_specs=[block, block, pl.BlockSpec((STEP, RANK), lambda i: (i, 0))],
     )(momentum_ref, gradient_ref, basis_ref)
@@ -167,23 +167,23 @@
     )(me, *(pltpu.with_memory_space_constraint(x, pltpu.HBM) for x in args))
 
 
-def left_kernel(dims, high_ref, low_ref, factor_ref, *refs):
+def left_kernel(dims, tile, high_ref, low_ref, factor_ref, *refs):
     up_ref, down_ref = refs[-2:]
     half = down_ref.shape[0]
 
-    @pl.loop(0, 2 * half // TILE)
+    @pl.loop(0, 2 * half // tile)
     def _(c):
-        here = pl.ds(pl.multiple_of(c * TILE, TILE), TILE)
+        here = pl.ds(pl.multiple_of(c * tile, tile), tile)
         both = dot(high_ref[here, :], factor_ref[...], dims)
         fhigh = factor_ref[:HALF, :] if dims == NT else factor_ref[:, :HALF]
         part = (both[:, :HALF] + both[:, HALF:]) + dot(low_ref[here, :], fhigh, dims)
-        there = pl.ds(pl.multiple_of(lax.rem(c * TILE, half), TILE), TILE)
-
-        @pl.when(c < half // TILE)
+        there = pl.ds(pl.multiple_of(lax.rem(c * tile, half), tile), tile)
+
+        @pl.when(c < half // tile)
         def _():
             up_ref[there, :] = part
 
-        @pl.when(c >= half // TILE)
+        @pl.when(c >= half // tile)
         def _():
             down_ref[there, :] = part
 
@@ -191,10 +191,10 @@
         up_ref[half:, :] = refs[0][...]
 
 
-def left_product(buffer, factor, *square, dims=NT):
+def left_product(buffer, factor, *square, dims=NT, tile=TILE):
     rows, cols = buffer[0].shape
     return call(
-        functools.partial(left_kernel, dims), "left", 0, 4 * rows * cols,
+        functools.partial(left_kernel, dims, tile), "left", 0, 4 * rows * cols,
         out_shape=[shaped(rows // 2 + SUB * len(square), HALF), shaped(rows // 2, HALF)],
         in_specs=[VMEM] * (3 + len(square)), out_specs=[VMEM] * 2,
     )(*buffer, factor, *square)
@@ -259,7 +259,8 @@
 
 
 def first_kernel(me_ref, *refs):
-    blocks, (inverse_ref, wide_ref, out_ref, pair_ref, square_ref, gram_ref) = refs[:4], refs[4:]
+    halves, (inverse_ref, wide_ref, out_ref, pair_ref, square_ref, gram_ref) = refs[:2], refs[2:]
+    blocks = [ref.at[PART * b:PART * (b + 1), :] for ref in halves for b in range(2)]
     me = me_ref[0]
     place(gram_ref, me, [ref[:, :HALF] for ref in blocks])
     place(wide_ref, me, [ref[:, HALF:] for ref in blocks])
@@ -267,13 +268,13 @@
     square_ref[...] = solved(inverse_ref[...], wide_ref, out_ref, pair_ref)
 
 
-def first_solve(me, blocks):
-    cols = blocks[0].shape[1] - HALF
+def first_solve(me, mine, other):
+    cols = mine.shape[1] - HALF
     return call(
         first_kernel, "first_solve", 5_000_000_000, 20 * HALF * cols,
         out_shape=[shaped(HALF, HALF), shaped(HALF, cols), shaped(HALF, cols), shaped(RANK, cols, dtype=BF16), shaped(SUB, HALF)],
-        in_specs=[SMEM] + [VMEM] * 4, out_specs=[VMEM] * 5, scratch_shapes=[pltpu.VMEM((HALF, HALF), F32)],
-    )(me, *blocks)
+        in_specs=[SMEM] + [VMEM] * 2, out_specs=[VMEM] * 5, scratch_shapes=[pltpu.VMEM((HALF, HALF), F32)],
+    )(me, mine, other)
 
 
 def second_kernel(me_ref, *refs):
@@ -395,16 +396,16 @@
 
         total0 = side0 + cross0
         back0 = swap(total0, "row", 2)
-        others0 = swap(total0, "row", 1), swap(back0, "row", 1)
         side1 = part1[:PART] + jnp.concatenate(pair1, axis=0)
         cross1 = swap(side1, "row", 4)
-        total0, back0, others0, side1, cross1 = together(total0, back0, others0, side1, cross1)
-
+        total0, back0, side1, cross1 = together(total0, back0, side1, cross1)
+
+        mine0 = jnp.concatenate([total0, back0], axis=0)
         total1 = side1 + cross1
         back1, other1 = swap(total1, "row", 2), swap(total1, "row", 1)
-        first, wide, factor0, split0, square0 = first_solve(me, (total0, back0, *others0))
+        first, wide, factor0, split0, square0 = first_solve(me, mine0, swap(mine0, "row", 1))
         if not last:
-            up0, down0 = left_product(buffer, split0, square0)
+            up0, down0 = left_product(buffer, split0, square0, tile=STEP)
         total1, back1, other1, first, wide, split0, square0, up0, down0 = together(
             total1, back1, other1, first, wide, split0, square0, up0, down0
         )

time: 194 us -> 193 us (level)
  waiting for transfers between devices: 87.9 us -> 85.9 us
    ppermute x45 -> x43, waiting for transfers between devices: 87.9 us -> 85.9 us  [swap(): return lax.ppermute(x, axis, [(i, i ^ bit) for i in range(size)])]
    ppermute x45 -> x43, starting transfers between devices: 45.2 us -> 46 us  [swap(): return lax.ppermute(x, axis, [(i, i ^ bit) for i in range(size)])]
  transfers between devices with their start and end apart: 45 -> 43, of which waited for: 25 -> 26; matrix products, arithmetic and copies ran while one was open for 0% -> 0% of each run, Pallas kernels for 19% -> 19%
where the time goes in v3:
time: 193 us
  waiting for transfers between devices  85.9 us (45%)
  Pallas kernels  58.9 us (31%)
  starting transfers between devices  46 us (24%)
    ppermute x43, waiting for transfers between devices, swap(): return lax.ppermute(x, axis, [(i, i ^ bit) for i in range(size)])  85.9 us
    ppermute x43, starting transfers between devices, swap(): return lax.ppermute(x, axis, [(i, i ^ bit) for i in range(size)])  46 us
    pallas_call x2, Pallas kernels, second_solve(): call(second_kernel, 'second_solve', 6000000000, 20 * HALF * cols, out_sha...  12.5 us
    pallas_call x4, Pallas kernels, product(): call(functools.partial(product_kernel, not before, scaled), 'product', 4...  11.2 us
    pallas_call x2, Pallas kernels, first_solve(): call(first_kernel, 'first_solve', 5000000000, 20 * HALF * cols, out_shape...  10.4 us
    pallas_call x1, Pallas kernels, update(): call(update_kernel, 'update', 8 * rows * cols * RANK, 8 * rows * cols, ou...  8.78 us
    pallas_call x3, Pallas kernels, left_product(): call(functools.partial(left_kernel, dims, tile), 'left', 0, 4 * rows * co...  8.46 us
    pallas_call x1, Pallas kernels, start(): call(start_kernel, 'start', 4 * rows * cols * RANK, 6 * rows * cols, out_...  7.03 us
  transfers between devices with their start and end apart: 43, of which 26 were waited for; matrix products, arithmetic and copies ran while one was open for 0% of the time, Pallas kernels for 19%

profile of v3, /device:TPU:0, one launch (start us, length us, event | category | flops | bytes accessed | tf_op | source)
XLA Modules:
  0.0 192.6 jit_solution(17395751321880142614)
XLA Ops:
  0.6 7.0 %start.1 = (bf16[1024,2048]{1,0:T(8,128)(2,1)S(1)}, bf16[1024,2048]{1,0:T(8,128)(2,1)S(1)}, f32[512,128]{1,0:T(8,128)S(1)}, f32[512,128]{1,0:T(8,128)S(1)}, bf16[2048,256]{1,0:T(8,128)(2,1)S(1)}) custom-call(s32[1]{0:T(128)} %bitcast.me_ref, f32[1024,2048]{1,0:T(8,128)} %bitcast.6, bf16[1024,2048]{1,0:T(8,128)(2,1)} %bitcast.7, f32[2048,256]{1,0:T(8,128)} %basis_ref.1), custom_call_target="tpu_custom_call" | custom-call | flops 2147483648 | bytes 12582912 | tf_op jit(solution)/shard_map/start/pallas_call | solution.py:163
  7.7 3.0 %collective-permute-start = (f32[512,128]{1,0:T(8,128)S(1)}, f32[512,128]{1,0:T(8,128)S(1)}, u32[]{:S(2)}, u32[]{:S(2)}) collective-permute-start(f32[512,128]{1,0:T(8,128)S(1)} %get-tuple-element.132), channel_id=1, source_target_pairs={{0,1},{1,0},{2,3},{3,2},{4,5},{5,4},{6,7},{7,6},{8,9},{9,8},{10,11... | collective-permute-start | bytes 786440 | tf_op jit(solution)/shard_map/ppermute | solution.py:356
  12.2 2.9 %left.3 = (f32[512,128]{1,0:T(8,128)S(1)}, f32[512,128]{1,0:T(8,128)S(1)}) custom-call(bf16[1024,2048]{1,0:T(8,128)(2,1)S(1)} %get-tuple-element.127.high_ref.refs_4_.refs_5_, bf16[1024,2048]{1,0:T(8,128)(2,1)S(1)} %get-tuple-element.128.low_ref.refs_5_.refs_6_, bf16[2048,256]{1,0:T(8,128)(2,1)S(1)} %get-tuple-element.129.factor_ref), custom_call_target="tpu_custom_call" | custom-call | bytes 8388608 | tf_op jit(solution)/shard_map/left/pallas_call | solution.py:196
  20.7 4.7 %collective-permute-done.3.refs_3_ = f32[512,128]{1,0:T(8,128)S(1)} collective-permute-done((f32[512,128]{1,0:T(8,128)S(1)}, f32[512,128]{1,0:T(8,128)S(1)}, u32[]{:S(2)}, u32[]{:S(2)}) %collective-permute-start.3) | collective-permute-done | bytes 262176 | tf_op jit(solution)/shard_map/ppermute | solution.py:356
  37.7 4.8 %collective-permute-done.9.refs_4_ = f32[512,128]{1,0:T(8,128)S(1)} collective-permute-done((f32[512,128]{1,0:T(8,128)S(1)}, f32[512,128]{1,0:T(8,128)S(1)}, u32[]{:S(2)}, u32[]{:S(2)}) %collective-permute-start.9) | collective-permute-done | bytes 262176 | tf_op jit(solution)/shard_map/ppermute | solution.py:356
  42.9 3.5 %product.5 = (f32[64,2304]{1,0:T(8,128)S(1)}, f32[64,2304]{1,0:T(8,128)S(1)}, f32[1024,128]{1,0:T(8,128)}) custom-call(s32[1]{0:T(128)} %bitcast.me_ref, f32[1024,128]{1,0:T(8,128)S(1)} %get-tuple-element.149.refs_0_, f32[512,128]{1,0:T(8,128)S(1)} %add.67.refs_1_, f32[512,128]{1,0:T(8,128)S(1)} %collective-permute-done.8.refs_2_, ...), custom_call_target="tpu_custom_call" | custom-call | flops 2415919104 | bytes 9437184 | tf_op jit(solution)/shard_map/product/pallas_call | solution.py:240
  46.4 2.6 %collective-permute-start.10 = (f32[32,2176]{1,0:T(8,128)S(1)}, f32[32,2176]{1,0:T(8,128)S(1)}, u32[]{:S(2)}, u32[]{:S(2)}) collective-permute-start(f32[32,2176]{1,0:T(8,128)S(1)} %slice_add_fusion.1), channel_id=1, source_target_pairs={{0,16},{4,20},{8,24},{12,28},{16,0},{20,4},{24,8},{28,12},{1,17},{... | collective-permute-start | bytes 835592 | tf_op jit(solution)/shard_map/ppermute | solution.py:356
  51.2 11.3 %collective-permute-done.10 = f32[32,2176]{1,0:T(8,128)S(1)} collective-permute-done((f32[32,2176]{1,0:T(8,128)S(1)}, f32[32,2176]{1,0:T(8,128)S(1)}, u32[]{:S(2)}, u32[]{:S(2)}) %collective-permute-start.10) | collective-permute-done | bytes 278560 | tf_op jit(solution)/shard_map/ppermute | solution.py:356
  65.2 2.5 %collective-permute-start.14 = (f32[32,2176]{1,0:T(8,128)S(1)}, f32[32,2176]{1,0:T(8,128)S(1)}, u32[]{:S(2)}, u32[]{:S(2)}) collective-permute-start(f32[32,2176]{1,0:T(8,128)S(1)} %add.71), channel_id=1, source_target_pairs={{0,8},{4,12},{8,0},{12,4},{16,24},{20,28},{24,16},{28,20},{1,9},{5... | collective-permute-start | bytes 835592 | tf_op jit(solution)/shard_map/ppermute | solution.py:356
  67.8 8.8 %collective-permute-done.14 = f32[32,2176]{1,0:T(8,128)S(1)} collective-permute-done((f32[32,2176]{1,0:T(8,128)S(1)}, f32[32,2176]{1,0:T(8,128)S(1)}, u32[]{:S(2)}, u32[]{:S(2)}) %collective-permute-start.14) | collective-permute-done | bytes 278560 | tf_op jit(solution)/shard_map/ppermute | solution.py:356
  80.9 5.6 %first_solve.2 = (f32[128,128]{1,0:T(8,128)S(1)}, f32[128,2048]{1,0:T(8,128)S(1)}, f32[128,2048]{1,0:T(8,128)}, bf16[256,2048]{1,0:T(8,128)(2,1)S(1)}, f32[8,128]{1,0:T(8,128)S(1)}) custom-call(s32[1]{0:T(128)} %bitcast.me_ref, f32[64,2176]{1,0:T(8,128)S(1)} %constant_dynamic-update-slice_fusion.refs_0_, f32[64,2176]{1,0:T(8,128)S(1)} %collective-permute-done.18.refs_1_), custom_call_target="tpu_custom_call" | custom-call | flops 5000000000 | bytes 5242880 | tf_op jit(solution)/shard_map/first_solve/pallas_call | solution.py:273
  86.6 2.6 %left.4 = (f32[520,128]{1,0:T(8,128)S(1)}, f32[512,128]{1,0:T(8,128)S(1)}) custom-call(bf16[1024,2048]{1,0:T(8,128)(2,1)S(1)} %get-tuple-element.127.high_ref.refs_4_.refs_5_, bf16[1024,2048]{1,0:T(8,128)(2,1)S(1)} %get-tuple-element.128.low_ref.refs_5_.refs_6_, bf16[256,2048]{1,0:T(8,128)(2,1)S(1)} %get-tuple-element.171.factor_ref, ...), custom_call_target="tpu_custom_call" | custom-call | bytes 8388608 | tf_op jit(solution)/shard_map/left/pallas_call | solution.py:196
  92.3 6.6 %second_solve.2 = (f32[256,256]{1,0:T(8,128)}, f32[128,2048]{1,0:T(8,128)}, bf16[256,2048]{1,0:T(8,128)(2,1)S(1)}, f32[8,128]{1,0:T(8,128)S(1)}) custom-call(s32[1]{0:T(128)} %bitcast.me_ref, f32[32,2304]{1,0:T(8,128)S(1)} %add.73.refs_0_, f32[32,2304]{1,0:T(8,128)S(1)} %collective-permute-done.16.refs_1_, f32[32,2304]{1,0:T(8,128)S(1)} %collective-permute-done.17.refs_2_, ...), custom_call_target="tpu_custom_call" | custom-call | flops 6000000000 | bytes 5242880 | tf_op jit(solution)/shard_map/second_solve/pallas_call | solution.py:298
  101.2 3.0 %left.5 = (f32[520,128]{1,0:T(8,128)S(1)}, f32[512,128]{1,0:T(8,128)S(1)}) custom-call(bf16[1024,2048]{1,0:T(8,128)(2,1)S(1)} %get-tuple-element.127.high_ref.refs_4_.refs_5_, bf16[1024,2048]{1,0:T(8,128)(2,1)S(1)} %get-tuple-element.128.low_ref.refs_5_.refs_6_, bf16[256,2048]{1,0:T(8,128)(2,1)S(1)} %get-tuple-element.188.factor_ref, ...), custom_call_target="tpu_custom_call" | custom-call | bytes 8388608 | tf_op jit(solution)/shard_map/left/pallas_call | solution.py:196
  104.1 3.1 %collective-permute-done.23.refs_3_ = f32[512,128]{1,0:T(8,128)S(1)} collective-permute-done((f32[512,128]{1,0:T(8,128)S(1)}, f32[512,128]{1,0:T(8,128)S(1)}, u32[]{:S(2)}, u32[]{:S(2)}) %collective-permute-start.23) | collective-permute-done | bytes 262176 | tf_op jit(solution)/shard_map/ppermute | solution.py:356
  118.3 6.8 %collective-permute-done.27.refs_4_ = f32[512,128]{1,0:T(8,128)S(1)} collective-permute-done((f32[512,128]{1,0:T(8,128)S(1)}, f32[512,128]{1,0:T(8,128)S(1)}, u32[]{:S(2)}, u32[]{:S(2)}) %collective-permute-start.27) | collective-permute-done | bytes 262176 | tf_op jit(solution)/shard_map/ppermute | solution.py:356
  125.1 2.9 %product.7 = (f32[64,2304]{1,0:T(8,128)S(1)}, f32[64,2304]{1,0:T(8,128)S(1)}, f32[1024,128]{1,0:T(8,128)S(1)}) custom-call(s32[1]{0:T(128)} %bitcast.me_ref, f32[1024,128]{1,0:T(8,128)S(1)} %get-tuple-element.201.refs_0_.left0_ref, f32[520,128]{1,0:T(8,128)S(1)} %add.76.refs_1_, f32[520,128]{1,0:T(8,128)S(1)} %collective-permute-done.26.refs_2_, ...), custom_call_target="tpu_custom_call" | custom-call | flops 2415919104 | bytes 9437184 | tf_op jit(solution)/shard_map/product/pallas_call | solution.py:240
  132.3 11.8 %collective-permute-done.30 = f32[32,2176]{1,0:T(8,128)S(1)} collective-permute-done((f32[32,2176]{1,0:T(8,128)S(1)}, f32[32,2176]{1,0:T(8,128)S(1)}, u32[]{:S(2)}, u32[]{:S(2)}) %collective-permute-start.30) | collective-permute-done | bytes 278560 | tf_op jit(solution)/shard_map/ppermute | solution.py:356
  148.3 9.2 %collective-permute-done.34 = f32[32,2176]{1,0:T(8,128)S(1)} collective-permute-done((f32[32,2176]{1,0:T(8,128)S(1)}, f32[32,2176]{1,0:T(8,128)S(1)}, u32[]{:S(2)}, u32[]{:S(2)}) %collective-permute-start.34) | collective-permute-done | bytes 278560 | tf_op jit(solution)/shard_map/ppermute | solution.py:356
  157.5 3.2 %collective-permute-done.35 = f32[32,2304]{1,0:T(8,128)S(1)} collective-permute-done((f32[32,2304]{1,0:T(8,128)S(1)}, f32[32,2304]{1,0:T(8,128)S(1)}, u32[]{:S(2)}, u32[]{:S(2)}) %collective-permute-start.35) | collective-permute-done | bytes 294944 | tf_op jit(solution)/shard_map/ppermute | solution.py:356
  162.8 4.8 %first_solve.3 = (f32[128,128]{1,0:T(8,128)S(1)}, f32[128,2048]{1,0:T(8,128)S(1)}, f32[128,2048]{1,0:T(8,128)S(1)}, bf16[256,2048]{1,0:T(8,128)(2,1)S(1)}, f32[8,128]{1,0:T(8,128)S(1)}) custom-call(s32[1]{0:T(128)} %bitcast.me_ref, f32[64,2176]{1,0:T(8,128)S(1)} %constant_dynamic-update-slice_fusion.2.refs_0_, f32[64,2176]{1,0:T(8,128)S(1)} %collective-permute-done.38.refs_1_), custom_call_target="tpu_custom_call" | custom-call | flops 5000000000 | bytes 5242880 | tf_op jit(solution)/shard_map/first_solve/pallas_call | solution.py:273
  167.6 2.9 %collective-permute-done.36.refs_1_ = f32[32,2304]{1,0:T(8,128)S(1)} collective-permute-done((f32[32,2304]{1,0:T(8,128)S(1)}, f32[32,2304]{1,0:T(8,128)S(1)}, u32[]{:S(2)}, u32[]{:S(2)}) %collective-permute-start.36) | collective-permute-done | bytes 294944 | tf_op jit(solution)/shard_map/ppermute | solution.py:356
  172.0 5.9 %second_solve.3 = (f32[256,256]{1,0:T(8,128)S(1)}, f32[128,2048]{1,0:T(8,128)S(1)}, bf16[256,2048]{1,0:T(8,128)(2,1)S(1)}, f32[8,128]{1,0:T(8,128)S(1)}) custom-call(s32[1]{0:T(128)} %bitcast.me_ref, f32[32,2304]{1,0:T(8,128)S(1)} %add.83.refs_0_, f32[32,2304]{1,0:T(8,128)S(1)} %collective-permute-done.36.refs_1_, ...), custom_call_target="tpu_custom_call" | custom-call | flops 6000000000 | bytes 5242880 | tf_op jit(solution)/shard_map/second_solve/pallas_call | solution.py:298
  183.9 8.8 %update.1 = (f32[1024,2048]{1,0:T(8,128)}, f32[1024,2048]{1,0:T(8,128)}, f32[2048,256]{1,0:T(8,128)}) custom-call(f32[1024,256]{1,0:T(8,128)S(1)} %ortho.1.ortho_ref, f32[8,256]{1,0:T(8,128)S(1)} %constant_dynamic-update-slice_fusion.4.s0, f32[8,256]{1,0:T(8,128)S(1)} %collective-permute-done.40.s1, f32[8,256]{1,0:T(8,128)S(1)} %collective-permute-done.41.s2, ...), custom_call_target="tpu_custom_call" | custom-call | flops 4294967296 | bytes 16777216 | tf_op jit(solution)/shard_map/update/pallas_call | solution.py:346
  (111 shorter events, 63.6 us)
Async XLA Ops:
  7.7 9.3 %collective-permute-start = (f32[512,128]{1,0:T(8,128)S(1)}, f32[512,128]{1,0:T(8,128)S(1)}, u32[]{:S(2)}, u32[]{:S(2)}) collective-permute-start(f32[512,128]{1,0:T(8,128)S(1)} %get-tuple-element.132), channel_id=1, source_target_pairs={{0,1},{1,0},{2,3},{3,2},{4,5},{5,4},{6,7},{7,6},{8,9},{9,8},{10,11... | collective-permute-start | bytes 786440 | tf_op jit(solution)/shard_map/ppermute | solution.py:356
  33.6 8.8 %collective-permute-start.9 = (f32[512,128]{1,0:T(8,128)S(1)}, f32[512,128]{1,0:T(8,128)S(1)}, u32[]{:S(2)}, u32[]{:S(2)}) collective-permute-start(f32[512,128]{1,0:T(8,128)S(1)} %add.68.refs_3_), channel_id=1, source_target_pairs={{0,1},{1,0},{2,3},{3,2},{4,5},{5,4},{6,7},{7,6},{8,9},{9,8},{10,11... | collective-permute-start | bytes 786440 | tf_op jit(solution)/shard_map/ppermute | solution.py:356
  34.4 8.5 %collective-permute-start.8 = (f32[512,128]{1,0:T(8,128)S(1)}, f32[512,128]{1,0:T(8,128)S(1)}, u32[]{:S(2)}, u32[]{:S(2)}) collective-permute-start(f32[512,128]{1,0:T(8,128)S(1)} %add.67.refs_1_), channel_id=1, source_target_pairs={{0,2},{1,3},{2,0},{3,1},{4,6},{5,7},{6,4},{7,5},{8,10},{9,11},{10,... | collective-permute-start | bytes 786440 | tf_op jit(solution)/shard_map/ppermute | solution.py:356
  36.0 10.4 %collective-permute-start.7 = (f32[32,2176]{1,0:T(8,128)S(1)}, f32[32,2176]{1,0:T(8,128)S(1)}, u32[]{:S(2)}, u32[]{:S(2)}) collective-permute-start(f32[32,2176]{1,0:T(8,128)S(1)} %slice.40), channel_id=1, source_target_pairs={{0,8},{4,12},{8,0},{12,4},{16,24},{20,28},{24,16},{28,20},{1,9},{5... | collective-permute-start | bytes 835592 | tf_op jit(solution)/shard_map/ppermute | solution.py:356
  46.4 16.1 %collective-permute-start.10 = (f32[32,2176]{1,0:T(8,128)S(1)}, f32[32,2176]{1,0:T(8,128)S(1)}, u32[]{:S(2)}, u32[]{:S(2)}) collective-permute-start(f32[32,2176]{1,0:T(8,128)S(1)} %slice_add_fusion.1), channel_id=1, source_target_pairs={{0,16},{4,20},{8,24},{12,28},{16,0},{20,4},{24,8},{28,12},{1,17},{... | collective-permute-start | bytes 835592 | tf_op jit(solution)/shard_map/ppermute | solution.py:356
  49.1 13.4 %collective-permute-start.13 = (f32[16,2304]{1,0:T(8,128)S(1)}, f32[16,2304]{1,0:T(8,128)S(1)}, u32[]{:S(2)}, u32[]{:S(2)}) collective-permute-start(f32[16,2304]{1,0:T(8,128)S(1)} %get-tuple-element.249), channel_id=1, source_target_pairs={{0,8},{4,12},{8,0},{12,4},{16,24},{20,28},{24,16},{28,20},{1,9},{5... | collective-permute-start | bytes 442376 | tf_op jit(solution)/shard_map/ppermute | solution.py:356
  50.7 12.5 %collective-permute-start.12 = (f32[16,2304]{1,0:T(8,128)S(1)}, f32[16,2304]{1,0:T(8,128)S(1)}, u32[]{:S(2)}, u32[]{:S(2)}) collective-permute-start(f32[16,2304]{1,0:T(8,128)S(1)} %get-tuple-element.250), channel_id=1, source_target_pairs={{0,8},{4,12},{8,0},{12,4},{16,24},{20,28},{24,16},{28,20},{1,9},{5... | collective-permute-start | bytes 442376 | tf_op jit(solution)/shard_map/ppermute | solution.py:356
  63.3 15.6 %collective-permute-start.15 = (f32[32,2304]{1,0:T(8,128)S(1)}, f32[32,2304]{1,0:T(8,128)S(1)}, u32[]{:S(2)}, u32[]{:S(2)}) collective-permute-start(f32[32,2304]{1,0:T(8,128)S(1)} %maximum_add_fusion), channel_id=1, source_target_pairs={{0,16},{4,20},{8,24},{12,28},{16,0},{20,4},{24,8},{28,12},{1,17},{... | collective-permute-start | bytes 884744 | tf_op jit(solution)/shard_map/ppermute | solution.py:356
  65.2 11.4 %collective-permute-start.14 = (f32[32,2176]{1,0:T(8,128)S(1)}, f32[32,2176]{1,0:T(8,128)S(1)}, u32[]{:S(2)}, u32[]{:S(2)}) collective-permute-start(f32[32,2176]{1,0:T(8,128)S(1)} %add.71), channel_id=1, source_target_pairs={{0,8},{4,12},{8,0},{12,4},{16,24},{20,28},{24,16},{28,20},{1,9},{5... | collective-permute-start | bytes 835592 | tf_op jit(solution)/shard_map/ppermute | solution.py:356
  79.0 10.2 %collective-permute-start.17 = (f32[32,2304]{1,0:T(8,128)S(1)}, f32[32,2304]{1,0:T(8,128)S(1)}, u32[]{:S(2)}, u32[]{:S(2)}) collective-permute-start(f32[32,2304]{1,0:T(8,128)S(1)} %add.73.refs_0_), channel_id=1, source_target_pairs={{0,4},{4,0},{8,12},{12,8},{16,20},{20,16},{24,28},{28,24},{1,5},{5... | collective-permute-start | bytes 884744 | tf_op jit(solution)/shard_map/ppermute | solution.py:356
  79.6 9.6 %collective-permute-start.16 = (f32[32,2304]{1,0:T(8,128)S(1)}, f32[32,2304]{1,0:T(8,128)S(1)}, u32[]{:S(2)}, u32[]{:S(2)}) collective-permute-start(f32[32,2304]{1,0:T(8,128)S(1)} %add.73.refs_0_), channel_id=1, source_target_pairs={{0,8},{4,12},{8,0},{12,4},{16,24},{20,28},{24,16},{28,20},{1,9},{5... | collective-permute-start | bytes 884744 | tf_op jit(solution)/shard_map/ppermute | solution.py:356
  89.4 9.5 %collective-permute-start.20 = (f32[512,128]{1,0:T(8,128)S(1)}, f32[512,128]{1,0:T(8,128)S(1)}, u32[]{:S(2)}, u32[]{:S(2)}) collective-permute-start(f32[512,128]{1,0:T(8,128)S(1)} %get-tuple-element.186), channel_id=1, source_target_pairs={{0,2},{1,3},{2,0},{3,1},{4,6},{5,7},{6,4},{7,5},{8,10},{9,11},{10,... | collective-permute-start | bytes 786440 | tf_op jit(solution)/shard_map/ppermute | solution.py:356
  90.9 8.4 %collective-permute-start.19 = (f32[520,128]{1,0:T(8,128)S(1)}, f32[520,128]{1,0:T(8,128)S(1)}, u32[]{:S(2)}, u32[]{:S(2)}) collective-permute-start(f32[520,128]{1,0:T(8,128)S(1)} %get-tuple-element.184), channel_id=1, source_target_pairs={{0,1},{1,0},{2,3},{3,2},{4,5},{5,4},{6,7},{7,6},{8,9},{9,8},{10,11... | collective-permute-start | bytes 798728 | tf_op jit(solution)/shard_map/ppermute | solution.py:356
  99.3 7.9 %collective-permute-start.22 = (f32[520,128]{1,0:T(8,128)S(1)}, f32[520,128]{1,0:T(8,128)S(1)}, u32[]{:S(2)}, u32[]{:S(2)}) collective-permute-start(f32[520,128]{1,0:T(8,128)S(1)} %add.74.refs_0_), channel_id=1, source_target_pairs={{0,2},{1,3},{2,0},{3,1},{4,6},{5,7},{6,4},{7,5},{8,10},{9,11},{10,... | collective-permute-start | bytes 798728 | tf_op jit(solution)/shard_map/ppermute | solution.py:356
  107.2 7.8 %collective-permute-start.24 = (f32[520,128]{1,0:T(8,128)S(1)}, f32[520,128]{1,0:T(8,128)S(1)}, u32[]{:S(2)}, u32[]{:S(2)}) collective-permute-start(f32[520,128]{1,0:T(8,128)S(1)} %get-tuple-element.202), channel_id=1, source_target_pairs={{0,1},{1,0},{2,3},{3,2},{4,5},{5,4},{6,7},{7,6},{8,9},{9,8},{10,11... | collective-permute-start | bytes 798728 | tf_op jit(solution)/shard_map/ppermute | solution.py:356
  115.0 10.1 %collective-permute-start.26 = (f32[520,128]{1,0:T(8,128)S(1)}, f32[520,128]{1,0:T(8,128)S(1)}, u32[]{:S(2)}, u32[]{:S(2)}) collective-permute-start(f32[520,128]{1,0:T(8,128)S(1)} %add.76.refs_1_), channel_id=1, source_target_pairs={{0,2},{1,3},{2,0},{3,1},{4,6},{5,7},{6,4},{7,5},{8,10},{9,11},{10,... | collective-permute-start | bytes 798728 | tf_op jit(solution)/shard_map/ppermute | solution.py:356
  116.6 8.5 %collective-permute-start.27 = (f32[512,128]{1,0:T(8,128)S(1)}, f32[512,128]{1,0:T(8,128)S(1)}, u32[]{:S(2)}, u32[]{:S(2)}) collective-permute-start(f32[512,128]{1,0:T(8,128)S(1)} %add.77.refs_3_), channel_id=1, source_target_pairs={{0,1},{1,0},{2,3},{3,2},{4,5},{5,4},{6,7},{7,6},{8,9},{9,8},{10,11... | collective-permute-start | bytes 786440 | tf_op jit(solution)/shard_map/ppermute | solution.py:356
  117.6 10.4 %collective-permute-start.29 = (f32[32,2176]{1,0:T(8,128)S(1)}, f32[32,2176]{1,0:T(8,128)S(1)}, u32[]{:S(2)}, u32[]{:S(2)}) collective-permute-start(f32[32,2176]{1,0:T(8,128)S(1)} %slice.43), channel_id=1, source_target_pairs={{0,8},{4,12},{8,0},{12,4},{16,24},{20,28},{24,16},{28,20},{1,9},{5... | collective-permute-start | bytes 835592 | tf_op jit(solution)/shard_map/ppermute | solution.py:356
  128.1 16.1 %collective-permute-start.30 = (f32[32,2176]{1,0:T(8,128)S(1)}, f32[32,2176]{1,0:T(8,128)S(1)}, u32[]{:S(2)}, u32[]{:S(2)}) collective-permute-start(f32[32,2176]{1,0:T(8,128)S(1)} %slice_add_fusion), channel_id=1, source_target_pairs={{0,16},{4,20},{8,24},{12,28},{16,0},{20,4},{24,8},{28,12},{1,17},{... | collective-permute-start | bytes 835592 | tf_op jit(solution)/shard_map/ppermute | solution.py:356
  130.3 13.9 %collective-permute-start.33 = (f32[16,2304]{1,0:T(8,128)S(1)}, f32[16,2304]{1,0:T(8,128)S(1)}, u32[]{:S(2)}, u32[]{:S(2)}) collective-permute-start(f32[16,2304]{1,0:T(8,128)S(1)} %get-tuple-element.247), channel_id=1, source_target_pairs={{0,8},{4,12},{8,0},{12,4},{16,24},{20,28},{24,16},{28,20},{1,9},{5... | collective-permute-start | bytes 442376 | tf_op jit(solution)/shard_map/ppermute | solution.py:356
  131.6 13.5 %collective-permute-start.32 = (f32[16,2304]{1,0:T(8,128)S(1)}, f32[16,2304]{1,0:T(8,128)S(1)}, u32[]{:S(2)}, u32[]{:S(2)}) collective-permute-start(f32[16,2304]{1,0:T(8,128)S(1)} %get-tuple-element.248), channel_id=1, source_target_pairs={{0,8},{4,12},{8,0},{12,4},{16,24},{20,28},{24,16},{28,20},{1,9},{5... | collective-permute-start | bytes 442376 | tf_op jit(solution)/shard_map/ppermute | solution.py:356
  145.1 15.6 %collective-permute-start.35 = (f32[32,2304]{1,0:T(8,128)S(1)}, f32[32,2304]{1,0:T(8,128)S(1)}, u32[]{:S(2)}, u32[]{:S(2)}) collective-permute-start(f32[32,2304]{1,0:T(8,128)S(1)} %maximum_add_fusion.1), channel_id=1, source_target_pairs={{0,16},{4,20},{8,24},{12,28},{16,0},{20,4},{24,8},{28,12},{1,17},{... | collective-permute-start | bytes 884744 | tf_op jit(solution)/shard_map/ppermute | solution.py:356
  145.8 11.8 %collective-permute-start.34 = (f32[32,2176]{1,0:T(8,128)S(1)}, f32[32,2176]{1,0:T(8,128)S(1)}, u32[]{:S(2)}, u32[]{:S(2)}) collective-permute-start(f32[32,2176]{1,0:T(8,128)S(1)} %add.81), channel_id=1, source_target_pairs={{0,8},{4,12},{8,0},{12,4},{16,24},{20,28},{24,16},{28,20},{1,9},{5... | collective-permute-start | bytes 835592 | tf_op jit(solution)/shard_map/ppermute | solution.py:356
  161.4 9.0 %collective-permute-start.36 = (f32[32,2304]{1,0:T(8,128)S(1)}, f32[32,2304]{1,0:T(8,128)S(1)}, u32[]{:S(2)}, u32[]{:S(2)}) collective-permute-start(f32[32,2304]{1,0:T(8,128)S(1)} %add.83.refs_0_), channel_id=1, source_target_pairs={{0,8},{4,12},{8,0},{12,4},{16,24},{20,28},{24,16},{28,20},{1,9},{5... | collective-permute-start | bytes 884744 | tf_op jit(solution)/shard_map/ppermute | solution.py:356
  (21 other events, 112.0 us)

commit v4 on v3

--- a/solution.py
+++ b/solution.py
@@ -72,12 +72,10 @@
     def repeat(tile, sub):
         return jnp.broadcast_to(tile[sub:sub + 1, :], shape)
 
-    tiles = [block[SUB * i:SUB * (i + 1), :] for i in range(count)]
-    for t in range(count):
+    def pivot(t, tile):
         low = SUB * t
-        panel = jnp.logical_and(lanes >= low, lanes < low + SUB)
-        cols = [spread(tiles[t], low + j) for j in range(SUB)]
-        tile = jnp.where(panel, 0.0, tiles[t])
+        cols = [spread(tile, low + j) for j in range(SUB)]
+        tile = jnp.where(within(t), 0.0, tile)
         scale, rows, upper = [], [], {}
         for j in range(SUB):
             r = lax.rsqrt(repeat(cols[j], j))
@@ -89,16 +87,31 @@
             tile = jnp.where(subs == j, row, tile - mult * row)
             scale.append(r)
             rows.append(row)
-        tiles[t] = tile
-        for i in range(t + 1, count):
-            cols = [spread(tiles[i], low + j) for j in range(SUB)]
-            tile = jnp.where(panel, 0.0, tiles[i])
-            for j in range(SUB):
-                mult = cols[j] * scale[j]
-                for k in range(j + 1, SUB):
-                    cols[k] = cols[k] - mult * upper[j, k]
-                tile = tile - mult * rows[j]
-            tiles[i] = tile
+        return tile, (t, scale, rows, upper)
+
+    def eliminate(tile, t, scale, rows, upper):
+        cols = [spread(tile, SUB * t + j) for j in range(SUB)]
+        tile = jnp.where(within(t), 0.0, tile)
+        for j in range(SUB):
+            mult = cols[j] * scale[j]
+            for k in range(j + 1, SUB):
+                cols[k] = cols[k] - mult * upper[j, k]
+            tile = tile - mult * rows[j]
+        return tile
+
+    def within(t):
+        return jnp.logical_and(lanes >= SUB * t, lanes < SUB * (t + 1))
+
+    tiles = [block[SUB * i:SUB * (i + 1), :] for i in range(count)]
+    before = None
+    for t in range(count):
+        if before is not None:
+            tiles[t] = eliminate(tiles[t], *before)
+        tiles[t], panel = pivot(t, tiles[t])
+        if before is not None:
+            for i in range(t + 1, count):
+                tiles[i] = eliminate(tiles[i], *before)
+        before = panel
     full = jnp.concatenate(tiles, axis=0)
     down = lax.broadcasted_iota(jnp.int32, (HALF, HALF), 0)
     across = lax.broadcasted_iota(jnp.int32, (HALF, HALF), 1)

time: 193 us -> 193 us (level)
  no operation moved by 1% of the time
where the time goes in v4:
time: 193 us
  waiting for transfers between devices  85.9 us (45%)
  Pallas kernels  58.9 us (31%)
  starting transfers between devices  46 us (24%)
    ppermute x43, waiting for transfers between devices, swap(): return lax.ppermute(x, axis, [(i, i ^ bit) for i in range(size)])  85.9 us
    ppermute x43, starting transfers between devices, swap(): return lax.ppermute(x, axis, [(i, i ^ bit) for i in range(size)])  46 us
    pallas_call x2, Pallas kernels, second_solve(): call(second_kernel, 'second_solve', 6000000000, 20 * HALF * cols, out_sha...  12.5 us
    pallas_call x4, Pallas kernels, product(): call(functools.partial(product_kernel, not before, scaled), 'product', 4...  11.2 us
    pallas_call x2, Pallas kernels, first_solve(): call(first_kernel, 'first_solve', 5000000000, 20 * HALF * cols, out_shape...  10.4 us
    pallas_call x1, Pallas kernels, update(): call(update_kernel, 'update', 8 * rows * cols * RANK, 8 * rows * cols, ou...  8.78 us
    pallas_call x3, Pallas kernels, left_product(): call(functools.partial(left_kernel, dims, tile), 'left', 0, 4 * rows * co...  8.47 us
    pallas_call x1, Pallas kernels, start(): call(start_kernel, 'start', 4 * rows * cols * RANK, 6 * rows * cols, out_...  7.03 us
  transfers between devices with their start and end apart: 43, of which 26 were waited for; matrix products, arithmetic and copies ran while one was open for 0% of the time, Pallas kernels for 19%

profile of v4, /device:TPU:0, one launch (start us, length us, event | category | flops | bytes accessed | tf_op | source)
XLA Modules:
  0.0 192.6 jit_solution(14938429369228851757)
XLA Ops:
  0.6 7.0 %start.1 = (bf16[1024,2048]{1,0:T(8,128)(2,1)S(1)}, bf16[1024,2048]{1,0:T(8,128)(2,1)S(1)}, f32[512,128]{1,0:T(8,128)S(1)}, f32[512,128]{1,0:T(8,128)S(1)}, bf16[2048,256]{1,0:T(8,128)(2,1)S(1)}) custom-call(s32[1]{0:T(128)} %bitcast.me_ref, f32[1024,2048]{1,0:T(8,128)} %bitcast.6, bf16[1024,2048]{1,0:T(8,128)(2,1)} %bitcast.7, f32[2048,256]{1,0:T(8,128)} %basis_ref.1), custom_call_target="tpu_custom_call" | custom-call | flops 2147483648 | bytes 12582912 | tf_op jit(solution)/shard_map/start/pallas_call | solution.py:176
  7.7 3.0 %collective-permute-start = (f32[512,128]{1,0:T(8,128)S(1)}, f32[512,128]{1,0:T(8,128)S(1)}, u32[]{:S(2)}, u32[]{:S(2)}) collective-permute-start(f32[512,128]{1,0:T(8,128)S(1)} %get-tuple-element.132), channel_id=1, source_target_pairs={{0,1},{1,0},{2,3},{3,2},{4,5},{5,4},{6,7},{7,6},{8,9},{9,8},{10,11... | collective-permute-start | bytes 786440 | tf_op jit(solution)/shard_map/ppermute | solution.py:369
  12.2 2.9 %left.3 = (f32[512,128]{1,0:T(8,128)S(1)}, f32[512,128]{1,0:T(8,128)S(1)}) custom-call(bf16[1024,2048]{1,0:T(8,128)(2,1)S(1)} %get-tuple-element.127.high_ref.refs_4_.refs_5_, bf16[1024,2048]{1,0:T(8,128)(2,1)S(1)} %get-tuple-element.128.low_ref.refs_5_.refs_6_, bf16[2048,256]{1,0:T(8,128)(2,1)S(1)} %get-tuple-element.129.factor_ref), custom_call_target="tpu_custom_call" | custom-call | bytes 8388608 | tf_op jit(solution)/shard_map/left/pallas_call | solution.py:209
  20.7 4.7 %collective-permute-done.3.refs_3_ = f32[512,128]{1,0:T(8,128)S(1)} collective-permute-done((f32[512,128]{1,0:T(8,128)S(1)}, f32[512,128]{1,0:T(8,128)S(1)}, u32[]{:S(2)}, u32[]{:S(2)}) %collective-permute-start.3) | collective-permute-done | bytes 262176 | tf_op jit(solution)/shard_map/ppermute | solution.py:369
  37.7 4.8 %collective-permute-done.9.refs_4_ = f32[512,128]{1,0:T(8,128)S(1)} collective-permute-done((f32[512,128]{1,0:T(8,128)S(1)}, f32[512,128]{1,0:T(8,128)S(1)}, u32[]{:S(2)}, u32[]{:S(2)}) %collective-permute-start.9) | collective-permute-done | bytes 262176 | tf_op jit(solution)/shard_map/ppermute | solution.py:369
  42.9 3.5 %product.5 = (f32[64,2304]{1,0:T(8,128)S(1)}, f32[64,2304]{1,0:T(8,128)S(1)}, f32[1024,128]{1,0:T(8,128)}) custom-call(s32[1]{0:T(128)} %bitcast.me_ref, f32[1024,128]{1,0:T(8,128)S(1)} %get-tuple-element.149.refs_0_, f32[512,128]{1,0:T(8,128)S(1)} %add.67.refs_1_, f32[512,128]{1,0:T(8,128)S(1)} %collective-permute-done.8.refs_2_, ...), custom_call_target="tpu_custom_call" | custom-call | flops 2415919104 | bytes 9437184 | tf_op jit(solution)/shard_map/product/pallas_call | solution.py:253
  46.4 2.6 %collective-permute-start.10 = (f32[32,2176]{1,0:T(8,128)S(1)}, f32[32,2176]{1,0:T(8,128)S(1)}, u32[]{:S(2)}, u32[]{:S(2)}) collective-permute-start(f32[32,2176]{1,0:T(8,128)S(1)} %slice_add_fusion.1), channel_id=1, source_target_pairs={{0,16},{4,20},{8,24},{12,28},{16,0},{20,4},{24,8},{28,12},{1,17},{... | collective-permute-start | bytes 835592 | tf_op jit(solution)/shard_map/ppermute | solution.py:369
  51.2 11.3 %collective-permute-done.10 = f32[32,2176]{1,0:T(8,128)S(1)} collective-permute-done((f32[32,2176]{1,0:T(8,128)S(1)}, f32[32,2176]{1,0:T(8,128)S(1)}, u32[]{:S(2)}, u32[]{:S(2)}) %collective-permute-start.10) | collective-permute-done | bytes 278560 | tf_op jit(solution)/shard_map/ppermute | solution.py:369
  65.2 2.5 %collective-permute-start.14 = (f32[32,2176]{1,0:T(8,128)S(1)}, f32[32,2176]{1,0:T(8,128)S(1)}, u32[]{:S(2)}, u32[]{:S(2)}) collective-permute-start(f32[32,2176]{1,0:T(8,128)S(1)} %add.71), channel_id=1, source_target_pairs={{0,8},{4,12},{8,0},{12,4},{16,24},{20,28},{24,16},{28,20},{1,9},{5... | collective-permute-start | bytes 835592 | tf_op jit(solution)/shard_map/ppermute | solution.py:369
  67.8 8.8 %collective-permute-done.14 = f32[32,2176]{1,0:T(8,128)S(1)} collective-permute-done((f32[32,2176]{1,0:T(8,128)S(1)}, f32[32,2176]{1,0:T(8,128)S(1)}, u32[]{:S(2)}, u32[]{:S(2)}) %collective-permute-start.14) | collective-permute-done | bytes 278560 | tf_op jit(solution)/shard_map/ppermute | solution.py:369
  80.9 5.6 %first_solve.2 = (f32[128,128]{1,0:T(8,128)S(1)}, f32[128,2048]{1,0:T(8,128)S(1)}, f32[128,2048]{1,0:T(8,128)}, bf16[256,2048]{1,0:T(8,128)(2,1)S(1)}, f32[8,128]{1,0:T(8,128)S(1)}) custom-call(s32[1]{0:T(128)} %bitcast.me_ref, f32[64,2176]{1,0:T(8,128)S(1)} %constant_dynamic-update-slice_fusion.refs_0_, f32[64,2176]{1,0:T(8,128)S(1)} %collective-permute-done.18.refs_1_), custom_call_target="tpu_custom_call" | custom-call | flops 5000000000 | bytes 5242880 | tf_op jit(solution)/shard_map/first_solve/pallas_call | solution.py:286
  86.6 2.6 %left.4 = (f32[520,128]{1,0:T(8,128)S(1)}, f32[512,128]{1,0:T(8,128)S(1)}) custom-call(bf16[1024,2048]{1,0:T(8,128)(2,1)S(1)} %get-tuple-element.127.high_ref.refs_4_.refs_5_, bf16[1024,2048]{1,0:T(8,128)(2,1)S(1)} %get-tuple-element.128.low_ref.refs_5_.refs_6_, bf16[256,2048]{1,0:T(8,128)(2,1)S(1)} %get-tuple-element.171.factor_ref, ...), custom_call_target="tpu_custom_call" | custom-call | bytes 8388608 | tf_op jit(solution)/shard_map/left/pallas_call | solution.py:209
  92.3 6.6 %second_solve.2 = (f32[256,256]{1,0:T(8,128)}, f32[128,2048]{1,0:T(8,128)}, bf16[256,2048]{1,0:T(8,128)(2,1)S(1)}, f32[8,128]{1,0:T(8,128)S(1)}) custom-call(s32[1]{0:T(128)} %bitcast.me_ref, f32[32,2304]{1,0:T(8,128)S(1)} %add.73.refs_0_, f32[32,2304]{1,0:T(8,128)S(1)} %collective-permute-done.16.refs_1_, f32[32,2304]{1,0:T(8,128)S(1)} %collective-permute-done.17.refs_2_, ...), custom_call_target="tpu_custom_call" | custom-call | flops 6000000000 | bytes 5242880 | tf_op jit(solution)/shard_map/second_solve/pallas_call | solution.py:311
  101.1 3.0 %left.5 = (f32[520,128]{1,0:T(8,128)S(1)}, f32[512,128]{1,0:T(8,128)S(1)}) custom-call(bf16[1024,2048]{1,0:T(8,128)(2,1)S(1)} %get-tuple-element.127.high_ref.refs_4_.refs_5_, bf16[1024,2048]{1,0:T(8,128)(2,1)S(1)} %get-tuple-element.128.low_ref.refs_5_.refs_6_, bf16[256,2048]{1,0:T(8,128)(2,1)S(1)} %get-tuple-element.188.factor_ref, ...), custom_call_target="tpu_custom_call" | custom-call | bytes 8388608 | tf_op jit(solution)/shard_map/left/pallas_call | solution.py:209
  104.1 3.0 %collective-permute-done.23.refs_3_ = f32[512,128]{1,0:T(8,128)S(1)} collective-permute-done((f32[512,128]{1,0:T(8,128)S(1)}, f32[512,128]{1,0:T(8,128)S(1)}, u32[]{:S(2)}, u32[]{:S(2)}) %collective-permute-start.23) | collective-permute-done | bytes 262176 | tf_op jit(solution)/shard_map/ppermute | solution.py:369
  118.3 6.8 %collective-permute-done.27.refs_4_ = f32[512,128]{1,0:T(8,128)S(1)} collective-permute-done((f32[512,128]{1,0:T(8,128)S(1)}, f32[512,128]{1,0:T(8,128)S(1)}, u32[]{:S(2)}, u32[]{:S(2)}) %collective-permute-start.27) | collective-permute-done | bytes 262176 | tf_op jit(solution)/shard_map/ppermute | solution.py:369
  125.1 2.9 %product.7 = (f32[64,2304]{1,0:T(8,128)S(1)}, f32[64,2304]{1,0:T(8,128)S(1)}, f32[1024,128]{1,0:T(8,128)S(1)}) custom-call(s32[1]{0:T(128)} %bitcast.me_ref, f32[1024,128]{1,0:T(8,128)S(1)} %get-tuple-element.201.refs_0_.left0_ref, f32[520,128]{1,0:T(8,128)S(1)} %add.76.refs_1_, f32[520,128]{1,0:T(8,128)S(1)} %collective-permute-done.26.refs_2_, ...), custom_call_target="tpu_custom_call" | custom-call | flops 2415919104 | bytes 9437184 | tf_op jit(solution)/shard_map/product/pallas_call | solution.py:253
  132.3 11.8 %collective-permute-done.30 = f32[32,2176]{1,0:T(8,128)S(1)} collective-permute-done((f32[32,2176]{1,0:T(8,128)S(1)}, f32[32,2176]{1,0:T(8,128)S(1)}, u32[]{:S(2)}, u32[]{:S(2)}) %collective-permute-start.30) | collective-permute-done | bytes 278560 | tf_op jit(solution)/shard_map/ppermute | solution.py:369
  148.3 9.2 %collective-permute-done.34 = f32[32,2176]{1,0:T(8,128)S(1)} collective-permute-done((f32[32,2176]{1,0:T(8,128)S(1)}, f32[32,2176]{1,0:T(8,128)S(1)}, u32[]{:S(2)}, u32[]{:S(2)}) %collective-permute-start.34) | collective-permute-done | bytes 278560 | tf_op jit(solution)/shard_map/ppermute | solution.py:369
  157.5 3.2 %collective-permute-done.35 = f32[32,2304]{1,0:T(8,128)S(1)} collective-permute-done((f32[32,2304]{1,0:T(8,128)S(1)}, f32[32,2304]{1,0:T(8,128)S(1)}, u32[]{:S(2)}, u32[]{:S(2)}) %collective-permute-start.35) | collective-permute-done | bytes 294944 | tf_op jit(solution)/shard_map/ppermute | solution.py:369
  162.7 4.8 %first_solve.3 = (f32[128,128]{1,0:T(8,128)S(1)}, f32[128,2048]{1,0:T(8,128)S(1)}, f32[128,2048]{1,0:T(8,128)S(1)}, bf16[256,2048]{1,0:T(8,128)(2,1)S(1)}, f32[8,128]{1,0:T(8,128)S(1)}) custom-call(s32[1]{0:T(128)} %bitcast.me_ref, f32[64,2176]{1,0:T(8,128)S(1)} %constant_dynamic-update-slice_fusion.2.refs_0_, f32[64,2176]{1,0:T(8,128)S(1)} %collective-permute-done.38.refs_1_), custom_call_target="tpu_custom_call" | custom-call | flops 5000000000 | bytes 5242880 | tf_op jit(solution)/shard_map/first_solve/pallas_call | solution.py:286
  167.5 2.9 %collective-permute-done.36.refs_1_ = f32[32,2304]{1,0:T(8,128)S(1)} collective-permute-done((f32[32,2304]{1,0:T(8,128)S(1)}, f32[32,2304]{1,0:T(8,128)S(1)}, u32[]{:S(2)}, u32[]{:S(2)}) %collective-permute-start.36) | collective-permute-done | bytes 294944 | tf_op jit(solution)/shard_map/ppermute | solution.py:369
  172.0 5.9 %second_solve.3 = (f32[256,256]{1,0:T(8,128)S(1)}, f32[128,2048]{1,0:T(8,128)S(1)}, bf16[256,2048]{1,0:T(8,128)(2,1)S(1)}, f32[8,128]{1,0:T(8,128)S(1)}) custom-call(s32[1]{0:T(128)} %bitcast.me_ref, f32[32,2304]{1,0:T(8,128)S(1)} %add.83.refs_0_, f32[32,2304]{1,0:T(8,128)S(1)} %collective-permute-done.36.refs_1_, ...), custom_call_target="tpu_custom_call" | custom-call | flops 6000000000 | bytes 5242880 | tf_op jit(solution)/shard_map/second_solve/pallas_call | solution.py:311
  183.8 8.8 %update.1 = (f32[1024,2048]{1,0:T(8,128)}, f32[1024,2048]{1,0:T(8,128)}, f32[2048,256]{1,0:T(8,128)}) custom-call(f32[1024,256]{1,0:T(8,128)S(1)} %ortho.1.ortho_ref, f32[8,256]{1,0:T(8,128)S(1)} %constant_dynamic-update-slice_fusion.4.s0, f32[8,256]{1,0:T(8,128)S(1)} %collective-permute-done.40.s1, f32[8,256]{1,0:T(8,128)S(1)} %collective-permute-done.41.s2, ...), custom_call_target="tpu_custom_call" | custom-call | flops 4294967296 | bytes 16777216 | tf_op jit(solution)/shard_map/update/pallas_call | solution.py:359
  (111 shorter events, 63.6 us)
Async XLA Ops:
  7.7 9.3 %collective-permute-start = (f32[512,128]{1,0:T(8,128)S(1)}, f32[512,128]{1,0:T(8,128)S(1)}, u32[]{:S(2)}, u32[]{:S(2)}) collective-permute-start(f32[512,128]{1,0:T(8,128)S(1)} %get-tuple-element.132), channel_id=1, source_target_pairs={{0,1},{1,0},{2,3},{3,2},{4,5},{5,4},{6,7},{7,6},{8,9},{9,8},{10,11... | collective-permute-start | bytes 786440 | tf_op jit(solution)/shard_map/ppermute | solution.py:369
  33.6 8.8 %collective-permute-start.9 = (f32[512,128]{1,0:T(8,128)S(1)}, f32[512,128]{1,0:T(8,128)S(1)}, u32[]{:S(2)}, u32[]{:S(2)}) collective-permute-start(f32[512,128]{1,0:T(8,128)S(1)} %add.68.refs_3_), channel_id=1, source_target_pairs={{0,1},{1,0},{2,3},{3,2},{4,5},{5,4},{6,7},{7,6},{8,9},{9,8},{10,11... | collective-permute-start | bytes 786440 | tf_op jit(solution)/shard_map/ppermute | solution.py:369
  34.4 8.5 %collective-permute-start.8 = (f32[512,128]{1,0:T(8,128)S(1)}, f32[512,128]{1,0:T(8,128)S(1)}, u32[]{:S(2)}, u32[]{:S(2)}) collective-permute-start(f32[512,128]{1,0:T(8,128)S(1)} %add.67.refs_1_), channel_id=1, source_target_pairs={{0,2},{1,3},{2,0},{3,1},{4,6},{5,7},{6,4},{7,5},{8,10},{9,11},{10,... | collective-permute-start | bytes 786440 | tf_op jit(solution)/shard_map/ppermute | solution.py:369
  36.0 10.4 %collective-permute-start.7 = (f32[32,2176]{1,0:T(8,128)S(1)}, f32[32,2176]{1,0:T(8,128)S(1)}, u32[]{:S(2)}, u32[]{:S(2)}) collective-permute-start(f32[32,2176]{1,0:T(8,128)S(1)} %slice.40), channel_id=1, source_target_pairs={{0,8},{4,12},{8,0},{12,4},{16,24},{20,28},{24,16},{28,20},{1,9},{5... | collective-permute-start | bytes 835592 | tf_op jit(solution)/shard_map/ppermute | solution.py:369
  46.4 16.1 %collective-permute-start.10 = (f32[32,2176]{1,0:T(8,128)S(1)}, f32[32,2176]{1,0:T(8,128)S(1)}, u32[]{:S(2)}, u32[]{:S(2)}) collective-permute-start(f32[32,2176]{1,0:T(8,128)S(1)} %slice_add_fusion.1), channel_id=1, source_target_pairs={{0,16},{4,20},{8,24},{12,28},{16,0},{20,4},{24,8},{28,12},{1,17},{... | collective-permute-start | bytes 835592 | tf_op jit(solution)/shard_map/ppermute | solution.py:369
  49.1 13.4 %collective-permute-start.13 = (f32[16,2304]{1,0:T(8,128)S(1)}, f32[16,2304]{1,0:T(8,128)S(1)}, u32[]{:S(2)}, u32[]{:S(2)}) collective-permute-start(f32[16,2304]{1,0:T(8,128)S(1)} %get-tuple-element.249), channel_id=1, source_target_pairs={{0,8},{4,12},{8,0},{12,4},{16,24},{20,28},{24,16},{28,20},{1,9},{5... | collective-permute-start | bytes 442376 | tf_op jit(solution)/shard_map/ppermute | solution.py:369
  50.7 12.5 %collective-permute-start.12 = (f32[16,2304]{1,0:T(8,128)S(1)}, f32[16,2304]{1,0:T(8,128)S(1)}, u32[]{:S(2)}, u32[]{:S(2)}) collective-permute-start(f32[16,2304]{1,0:T(8,128)S(1)} %get-tuple-element.250), channel_id=1, source_target_pairs={{0,8},{4,12},{8,0},{12,4},{16,24},{20,28},{24,16},{28,20},{1,9},{5... | collective-permute-start | bytes 442376 | tf_op jit(solution)/shard_map/ppermute | solution.py:369
  63.3 15.6 %collective-permute-start.15 = (f32[32,2304]{1,0:T(8,128)S(1)}, f32[32,2304]{1,0:T(8,128)S(1)}, u32[]{:S(2)}, u32[]{:S(2)}) collective-permute-start(f32[32,2304]{1,0:T(8,128)S(1)} %maximum_add_fusion), channel_id=1, source_target_pairs={{0,16},{4,20},{8,24},{12,28},{16,0},{20,4},{24,8},{28,12},{1,17},{... | collective-permute-start | bytes 884744 | tf_op jit(solution)/shard_map/ppermute | solution.py:369
  65.2 11.4 %collective-permute-start.14 = (f32[32,2176]{1,0:T(8,128)S(1)}, f32[32,2176]{1,0:T(8,128)S(1)}, u32[]{:S(2)}, u32[]{:S(2)}) collective-permute-start(f32[32,2176]{1,0:T(8,128)S(1)} %add.71), channel_id=1, source_target_pairs={{0,8},{4,12},{8,0},{12,4},{16,24},{20,28},{24,16},{28,20},{1,9},{5... | collective-permute-start | bytes 835592 | tf_op jit(solution)/shard_map/ppermute | solution.py:369
  79.0 10.1 %collective-permute-start.17 = (f32[32,2304]{1,0:T(8,128)S(1)}, f32[32,2304]{1,0:T(8,128)S(1)}, u32[]{:S(2)}, u32[]{:S(2)}) collective-permute-start(f32[32,2304]{1,0:T(8,128)S(1)} %add.73.refs_0_), channel_id=1, source_target_pairs={{0,4},{4,0},{8,12},{12,8},{16,20},{20,16},{24,28},{28,24},{1,5},{5... | collective-permute-start | bytes 884744 | tf_op jit(solution)/shard_map/ppermute | solution.py:369
  79.6 9.6 %collective-permute-start.16 = (f32[32,2304]{1,0:T(8,128)S(1)}, f32[32,2304]{1,0:T(8,128)S(1)}, u32[]{:S(2)}, u32[]{:S(2)}) collective-permute-start(f32[32,2304]{1,0:T(8,128)S(1)} %add.73.refs_0_), channel_id=1, source_target_pairs={{0,8},{4,12},{8,0},{12,4},{16,24},{20,28},{24,16},{28,20},{1,9},{5... | collective-permute-start | bytes 884744 | tf_op jit(solution)/shard_map/ppermute | solution.py:369
  89.4 9.5 %collective-permute-start.20 = (f32[512,128]{1,0:T(8,128)S(1)}, f32[512,128]{1,0:T(8,128)S(1)}, u32[]{:S(2)}, u32[]{:S(2)}) collective-permute-start(f32[512,128]{1,0:T(8,128)S(1)} %get-tuple-element.186), channel_id=1, source_target_pairs={{0,2},{1,3},{2,0},{3,1},{4,6},{5,7},{6,4},{7,5},{8,10},{9,11},{10,... | collective-permute-start | bytes 786440 | tf_op jit(solution)/shard_map/ppermute | solution.py:369
  90.8 8.4 %collective-permute-start.19 = (f32[520,128]{1,0:T(8,128)S(1)}, f32[520,128]{1,0:T(8,128)S(1)}, u32[]{:S(2)}, u32[]{:S(2)}) collective-permute-start(f32[520,128]{1,0:T(8,128)S(1)} %get-tuple-element.184), channel_id=1, source_target_pairs={{0,1},{1,0},{2,3},{3,2},{4,5},{5,4},{6,7},{7,6},{8,9},{9,8},{10,11... | collective-permute-start | bytes 798728 | tf_op jit(solution)/shard_map/ppermute | solution.py:369
  99.2 7.9 %collective-permute-start.22 = (f32[520,128]{1,0:T(8,128)S(1)}, f32[520,128]{1,0:T(8,128)S(1)}, u32[]{:S(2)}, u32[]{:S(2)}) collective-permute-start(f32[520,128]{1,0:T(8,128)S(1)} %add.74.refs_0_), channel_id=1, source_target_pairs={{0,2},{1,3},{2,0},{3,1},{4,6},{5,7},{6,4},{7,5},{8,10},{9,11},{10,... | collective-permute-start | bytes 798728 | tf_op jit(solution)/shard_map/ppermute | solution.py:369
  107.2 7.8 %collective-permute-start.24 = (f32[520,128]{1,0:T(8,128)S(1)}, f32[520,128]{1,0:T(8,128)S(1)}, u32[]{:S(2)}, u32[]{:S(2)}) collective-permute-start(f32[520,128]{1,0:T(8,128)S(1)} %get-tuple-element.202), channel_id=1, source_target_pairs={{0,1},{1,0},{2,3},{3,2},{4,5},{5,4},{6,7},{7,6},{8,9},{9,8},{10,11... | collective-permute-start | bytes 798728 | tf_op jit(solution)/shard_map/ppermute | solution.py:369
  115.0 10.1 %collective-permute-start.26 = (f32[520,128]{1,0:T(8,128)S(1)}, f32[520,128]{1,0:T(8,128)S(1)}, u32[]{:S(2)}, u32[]{:S(2)}) collective-permute-start(f32[520,128]{1,0:T(8,128)S(1)} %add.76.refs_1_), channel_id=1, source_target_pairs={{0,2},{1,3},{2,0},{3,1},{4,6},{5,7},{6,4},{7,5},{8,10},{9,11},{10,... | collective-permute-start | bytes 798728 | tf_op jit(solution)/shard_map/ppermute | solution.py:369
  116.5 8.5 %collective-permute-start.27 = (f32[512,128]{1,0:T(8,128)S(1)}, f32[512,128]{1,0:T(8,128)S(1)}, u32[]{:S(2)}, u32[]{:S(2)}) collective-permute-start(f32[512,128]{1,0:T(8,128)S(1)} %add.77.refs_3_), channel_id=1, source_target_pairs={{0,1},{1,0},{2,3},{3,2},{4,5},{5,4},{6,7},{7,6},{8,9},{9,8},{10,11... | collective-permute-start | bytes 786440 | tf_op jit(solution)/shard_map/ppermute | solution.py:369
  117.5 10.4 %collective-permute-start.29 = (f32[32,2176]{1,0:T(8,128)S(1)}, f32[32,2176]{1,0:T(8,128)S(1)}, u32[]{:S(2)}, u32[]{:S(2)}) collective-permute-start(f32[32,2176]{1,0:T(8,128)S(1)} %slice.43), channel_id=1, source_target_pairs={{0,8},{4,12},{8,0},{12,4},{16,24},{20,28},{24,16},{28,20},{1,9},{5... | collective-permute-start | bytes 835592 | tf_op jit(solution)/shard_map/ppermute | solution.py:369
  128.0 16.1 %collective-permute-start.30 = (f32[32,2176]{1,0:T(8,128)S(1)}, f32[32,2176]{1,0:T(8,128)S(1)}, u32[]{:S(2)}, u32[]{:S(2)}) collective-permute-start(f32[32,2176]{1,0:T(8,128)S(1)} %slice_add_fusion), channel_id=1, source_target_pairs={{0,16},{4,20},{8,24},{12,28},{16,0},{20,4},{24,8},{28,12},{1,17},{... | collective-permute-start | bytes 835592 | tf_op jit(solution)/shard_map/ppermute | solution.py:369
  130.2 13.9 %collective-permute-start.33 = (f32[16,2304]{1,0:T(8,128)S(1)}, f32[16,2304]{1,0:T(8,128)S(1)}, u32[]{:S(2)}, u32[]{:S(2)}) collective-permute-start(f32[16,2304]{1,0:T(8,128)S(1)} %get-tuple-element.247), channel_id=1, source_target_pairs={{0,8},{4,12},{8,0},{12,4},{16,24},{20,28},{24,16},{28,20},{1,9},{5... | collective-permute-start | bytes 442376 | tf_op jit(solution)/shard_map/ppermute | solution.py:369
  131.5 13.5 %collective-permute-start.32 = (f32[16,2304]{1,0:T(8,128)S(1)}, f32[16,2304]{1,0:T(8,128)S(1)}, u32[]{:S(2)}, u32[]{:S(2)}) collective-permute-start(f32[16,2304]{1,0:T(8,128)S(1)} %get-tuple-element.248), channel_id=1, source_target_pairs={{0,8},{4,12},{8,0},{12,4},{16,24},{20,28},{24,16},{28,20},{1,9},{5... | collective-permute-start | bytes 442376 | tf_op jit(solution)/shard_map/ppermute | solution.py:369
  145.1 15.6 %collective-permute-start.35 = (f32[32,2304]{1,0:T(8,128)S(1)}, f32[32,2304]{1,0:T(8,128)S(1)}, u32[]{:S(2)}, u32[]{:S(2)}) collective-permute-start(f32[32,2304]{1,0:T(8,128)S(1)} %maximum_add_fusion.1), channel_id=1, source_target_pairs={{0,16},{4,20},{8,24},{12,28},{16,0},{20,4},{24,8},{28,12},{1,17},{... | collective-permute-start | bytes 884744 | tf_op jit(solution)/shard_map/ppermute | solution.py:369
  145.7 11.8 %collective-permute-start.34 = (f32[32,2176]{1,0:T(8,128)S(1)}, f32[32,2176]{1,0:T(8,128)S(1)}, u32[]{:S(2)}, u32[]{:S(2)}) collective-permute-start(f32[32,2176]{1,0:T(8,128)S(1)} %add.81), channel_id=1, source_target_pairs={{0,8},{4,12},{8,0},{12,4},{16,24},{20,28},{24,16},{28,20},{1,9},{5... | collective-permute-start | bytes 835592 | tf_op jit(solution)/shard_map/ppermute | solution.py:369
  161.4 9.0 %collective-permute-start.36 = (f32[32,2304]{1,0:T(8,128)S(1)}, f32[32,2304]{1,0:T(8,128)S(1)}, u32[]{:S(2)}, u32[]{:S(2)}) collective-permute-start(f32[32,2304]{1,0:T(8,128)S(1)} %add.83.refs_0_), channel_id=1, source_target_pairs={{0,8},{4,12},{8,0},{12,4},{16,24},{20,28},{24,16},{28,20},{1,9},{5... | collective-permute-start | bytes 884744 | tf_op jit(solution)/shard_map/ppermute | solution.py:369
  (21 other events, 112.0 us)
